TPU v7x, 32 devices: a whole 2x2x4 slice. The times are simulated.
32 devices in a mesh: batch: 2 (over x), wide: 16 (over z, y, core).
Axes of the slice: x: 2, y: 2, z: 4, core: 2. Of those that a mesh axis runs over, the one named last changes fastest.
Arguments:
- prefix_in: bfloat16 [32, 1024, 2048], P(('batch', 'wide')), may hold values from -6 to 6
- action_in: bfloat16 [32, 256, 1024], P(('batch', 'wide')), may hold values from -6 to 6
- target: float32 [32, 256, 32], P(('batch', 'wide')), may hold values from -20 to 20
- valid_mask: int32 [32, 256, 32], P(('batch', 'wide')), may hold values from 0 to 1, as said below
- prefix_ids: int32 [32, 1024], P(('batch', 'wide')), may hold values from 0 to 1, never falling along the last dimension, each value on 1 to 1023 neighbouring positions
- action_ids: int32 [32, 256], P(('batch', 'wide')), may hold values from 0 to 1, never falling along the last dimension, each value on 1 to 255 neighbouring positions
- action_blocks: int32 [32, 256], P(('batch', 'wide')), may hold values 0 or 1
- learning_rate: float32 [1], replicated, may hold values from 1.4481547 to 2.8963094
- prefix_weight: float32 [2048, 512], P('wide'), may hold values from -0.125 to 0.125
- attention_weight: float32 [1024, 4608], P('wide'), may hold values from -0.1875 to 0.1875
- feedforward_weight: float32 [4096, 3, 1024], P('wide'), may hold values from -0.1875 to 0.1875
- prefix_gains: float32 [1, 2048], replicated, may hold values from -0.0625 to 0.0625
- action_gains: float32 [3, 1024], replicated, may hold values from -0.0625 to 0.0625
- readout_weight: float32 [1024, 32], replicated, may hold values from -0.1875 to 0.1875
- prefix_weight_moment: float32 [2048, 512], P('wide'), may hold values from -0.00390625 to 0.00390625
- attention_weight_moment: float32 [1024, 4608], P('wide'), may hold values from -0.00390625 to 0.00390625
- feedforward_weight_moment: float32 [4096, 3, 1024], P('wide'), may hold values from -0.00390625 to 0.00390625
- prefix_gains_moment: float32 [1, 2048], replicated, may hold values from -0.00390625 to 0.00390625
- action_gains_moment: float32 [3, 1024], replicated, may hold values from -0.00390625 to 0.00390625
- readout_weight_moment: float32 [1024, 32], replicated, may hold values from -0.00390625 to 0.00390625
- prefix_weight_average: float32 [2048, 512], P('wide'), may hold values from -0.125 to 0.125
- attention_weight_average: float32 [1024, 4608], P('wide'), may hold values from -0.1875 to 0.1875
- feedforward_weight_average: float32 [4096, 3, 1024], P('wide'), may hold values from -0.1875 to 0.1875
- prefix_gains_average: float32 [1, 2048], replicated, may hold values from -0.0625 to 0.0625
- action_gains_average: float32 [3, 1024], replicated, may hold values from -0.0625 to 0.0625
- readout_weight_average: float32 [1024, 32], replicated, may hold values from -0.1875 to 0.1875
Outputs:
- loss: float32 [], replicated
- prefix_weight_next: float32 [2048, 512], P('wide')
- attention_weight_next: float32 [1024, 4608], P('wide')
- feedforward_weight_next: float32 [4096, 3, 1024], P('wide')
- prefix_gains_next: float32 [1, 2048], replicated
- action_gains_next: float32 [3, 1024], replicated
- readout_weight_next: float32 [1024, 32], replicated
- prefix_weight_moment_next: float32 [2048, 512], P('wide')
- attention_weight_moment_next: float32 [1024, 4608], P('wide')
- feedforward_weight_moment_next: float32 [4096, 3, 1024], P('wide')
- prefix_gains_moment_next: float32 [1, 2048], replicated
- action_gains_moment_next: float32 [3, 1024], replicated
- readout_weight_moment_next: float32 [1024, 32], replicated
- prefix_weight_average_next: float32 [2048, 512], P('wide')
- attention_weight_average_next: float32 [1024, 4608], P('wide')
- feedforward_weight_average_next: float32 [4096, 3, 1024], P('wide')
- prefix_gains_average_next: float32 [1, 2048], replicated
- action_gains_average_next: float32 [3, 1024], replicated
- readout_weight_average_next: float32 [1024, 32], replicated
Inputs may be any that keep to these rules, and one draw needn't show every extreme that they name: prefix_ids: non-decreasing along each row; every episode number appears in both prefix_ids and action_ids of a row. action_ids: non-decreasing along each row; every episode number appears in both prefix_ids and action_ids of a row. valid_mask: 1 at every row's first action token.
All inputs are finite; a program needn't handle non-finite values. No bound on the sum of `action_blocks` on one device may be relied on, other than what follows from the above.
Results may differ from a plain program's by a relative error of at most 0.0058.
Values may be sent and summed in bfloat16 or wider, within the bound.
No kernel may reach another device: no remote copies, remote signals or barrier semaphores. Data moves between devices by JAX's collectives and lax.ppermute only.
A program may use at most 192 MiB of HBM per device.

v0:
```python
import jax
import jax.numpy as jnp
from jax import lax
from jax.sharding import PartitionSpec as P

HEADS = 8
HEAD_DIM = 256


NORM_EPSILON = 1e-06
MOMENTUM = 0.9
AVERAGE_DECAY = 0.8
NEGATIVE = -1e30


def rms_norm(stream, gain_row):
    return (
        stream
        * lax.rsqrt(jnp.mean(stream * stream, axis=-1, keepdims=True) + NORM_EPSILON)
        * (1.0 + gain_row)
    )


def norm_back(stream, gain_row, cotangent):
    _, pull = jax.vjp(rms_norm, stream, gain_row)
    return pull(cotangent)


def gated_unit(gate_value, linear_value):
    return jax.nn.gelu(gate_value, approximate=True) * linear_value


def visible(prefix_ids, action_ids, block_flags):
    levels = jnp.cumsum(block_flags)
    from_prefix = action_ids[:, None] == prefix_ids[None, :]
    from_action = (action_ids[:, None] == action_ids[None, :]) & (
        levels[None, :] <= levels[:, None]
    )
    return jnp.concatenate([from_prefix, from_action], axis=1).astype(jnp.int32)


def masked_scores(queries, key_rows, allowed):
    scores = jnp.einsum(
        "thd,kd->thk", queries, key_rows, preferred_element_type=jnp.float32
    ) * HEAD_DIM ** (-0.5)
    return jnp.where(allowed[:, None, :] != 0, scores, NEGATIVE)


def advance(weight, moment, average, gradient, step_rate):
    moment_next = MOMENTUM * moment + gradient
    weight_next = weight - step_rate * (gradient + MOMENTUM * moment_next)
    average_next = AVERAGE_DECAY * average + (1.0 - AVERAGE_DECAY) * weight_next
    return (weight_next, moment_next, average_next)


def on_device(
    prefix_in,
    action_in,
    target,
    valid_mask,
    prefix_ids,
    action_ids,
    action_blocks,
    learning_rate,
    prefix_weight,
    attention_weight,
    feedforward_weight,
    prefix_gains,
    action_gains,
    readout_weight,
    prefix_weight_moment,
    attention_weight_moment,
    feedforward_weight_moment,
    prefix_gains_moment,
    action_gains_moment,
    readout_weight_moment,
    prefix_weight_average,
    attention_weight_average,
    feedforward_weight_average,
    prefix_gains_average,
    action_gains_average,
    readout_weight_average,
):
    bf16 = jnp.bfloat16
    f32 = jnp.float32
    highest = lax.Precision.HIGHEST
    query_width = HEADS * HEAD_DIM
    qkv_width = query_width + 2 * HEAD_DIM
    score_scale = HEAD_DIM ** (-0.5)
    prefix_rows = prefix_in[0].astype(f32)
    action_rows = action_in[0].astype(f32)
    target_rows = target[0]
    valid_rows = valid_mask[0].astype(f32)
    allowed = visible(prefix_ids[0], action_ids[0], action_blocks[0])
    masters = (
        prefix_weight.astype(bf16),
        attention_weight.astype(bf16),
        feedforward_weight.astype(bf16),
    )
    prefix_full, attention_full, feedforward_full = (
        lax.all_gather(masters[0], "wide", axis=0, tiled=True),
        lax.all_gather(masters[1], "wide", axis=0, tiled=True),
        lax.all_gather(masters[2], "wide", axis=0, tiled=True),
    )
    prefix_norm = rms_norm(prefix_rows, prefix_gains[0]).astype(bf16)
    prefix_kv = jnp.dot(prefix_norm, prefix_full, preferred_element_type=f32).astype(bf16)
    action_norm = rms_norm(action_rows, action_gains[0]).astype(bf16)
    action_qkv = jnp.dot(
        action_norm, attention_full[:, :qkv_width], preferred_element_type=f32
    ).astype(bf16)
    queries = action_qkv[:, :query_width].reshape(-1, HEADS, HEAD_DIM)
    key_rows = jnp.concatenate(
        [prefix_kv[:, :HEAD_DIM], action_qkv[:, query_width : query_width + HEAD_DIM]], 0
    )
    value_rows = jnp.concatenate(
        [prefix_kv[:, HEAD_DIM:], action_qkv[:, query_width + HEAD_DIM :]], 0
    )
    scores = masked_scores(queries, key_rows, allowed)
    row_top = jnp.max(scores, axis=-1, keepdims=True)
    exp_scores = jnp.exp(scores - row_top)
    row_total = jnp.sum(exp_scores, axis=-1, keepdims=True)
    log_total = row_top + jnp.log(row_total)
    soft_weights = (exp_scores / row_total).astype(bf16)
    mixed_heads = jnp.einsum("thk,kd->thd", soft_weights, value_rows, preferred_element_type=f32)
    mixed_heads = mixed_heads.astype(bf16).reshape(-1, query_width)
    output_weight = attention_full[:, qkv_width:]
    residual = action_rows + jnp.einsum(
        "th,dh->td", mixed_heads, output_weight, preferred_element_type=f32
    )
    hidden_norm = rms_norm(residual, action_gains[1]).astype(bf16)
    gate_value = jnp.einsum(
        "td,fd->tf", hidden_norm, feedforward_full[:, 0], preferred_element_type=f32
    )
    linear_value = jnp.einsum(
        "td,fd->tf", hidden_norm, feedforward_full[:, 1], preferred_element_type=f32
    )
    hidden = gated_unit(gate_value, linear_value).astype(bf16)
    final_stream = residual + jnp.einsum(
        "tf,fd->td", hidden, feedforward_full[:, 2], preferred_element_type=f32
    )
    final_norm = rms_norm(final_stream, action_gains[2])
    predicted = jnp.dot(final_norm, readout_weight, precision=highest)
    error_term = predicted - target_rows
    loss_sum, valid_count = lax.psum(
        (jnp.sum(valid_rows * error_term * error_term), jnp.sum(valid_rows)), ("batch", "wide")
    )
    loss_value = loss_sum / valid_count
    back_predicted = 2.0 * valid_rows * error_term / valid_count
    grad_readout = jnp.dot(final_norm.T, back_predicted, precision=highest)
    back_final, grad_gain_final = norm_back(
        final_stream, action_gains[2], jnp.dot(back_predicted, readout_weight.T, precision=highest)
    )
    prefix_full, attention_full, feedforward_full = (
        lax.all_gather(masters[0], "wide", axis=0, tiled=True),
        lax.all_gather(masters[1], "wide", axis=0, tiled=True),
        lax.all_gather(masters[2], "wide", axis=0, tiled=True),
    )
    output_weight = attention_full[:, qkv_width:]
    back_branch = back_final.astype(bf16)
    back_hidden = jnp.einsum(
        "td,fd->tf", back_branch, feedforward_full[:, 2], preferred_element_type=f32
    )
    _, glu_pull = jax.vjp(gated_unit, gate_value, linear_value)
    back_gate, back_linear = glu_pull(back_hidden)
    back_gate = back_gate.astype(bf16)
    back_linear = back_linear.astype(bf16)
    back_norm_in = jnp.einsum(
        "tf,fd->td", back_gate, feedforward_full[:, 0], preferred_element_type=f32
    )
    back_norm_in = back_norm_in + jnp.einsum(
        "tf,fd->td", back_linear, feedforward_full[:, 1], preferred_element_type=f32
    )
    grad_feedforward = jnp.stack(
        [
            jnp.einsum("tf,td->fd", back_gate, hidden_norm, preferred_element_type=f32),
            jnp.einsum("tf,td->fd", back_linear, hidden_norm, preferred_element_type=f32),
            jnp.einsum("tf,td->fd", hidden, back_branch, preferred_element_type=f32),
        ],
        axis=1,
    )
    back_norm_out, grad_gain_hidden = norm_back(residual, action_gains[1], back_norm_in)
    back_residual = back_final + back_norm_out
    back_attention = back_residual.astype(bf16)
    grad_output = jnp.einsum("td,th->dh", back_attention, mixed_heads, preferred_element_type=f32)
    back_mixed = jnp.einsum("td,dh->th", back_attention, output_weight, preferred_element_type=f32)
    back_mixed = back_mixed.astype(bf16).reshape(-1, HEADS, HEAD_DIM)
    soft_again = jnp.exp(masked_scores(queries, key_rows, allowed) - log_total)
    back_soft = jnp.einsum("thd,kd->thk", back_mixed, value_rows, preferred_element_type=f32)
    back_scores = soft_again * (back_soft - jnp.sum(soft_again * back_soft, axis=-1, keepdims=True))
    back_scores = back_scores.astype(bf16)
    back_queries = (
        jnp.einsum("thk,kd->thd", back_scores, key_rows, preferred_element_type=f32) * score_scale
    )
    back_keys = (
        jnp.einsum("thk,thd->kd", back_scores, queries, preferred_element_type=f32) * score_scale
    )
    back_values = jnp.einsum(
        "thk,thd->kd", soft_again.astype(bf16), back_mixed, preferred_element_type=f32
    )
    prefix_length = prefix_kv.shape[0]
    back_qkv = jnp.concatenate(
        [
            back_queries.reshape(-1, query_width),
            back_keys[prefix_length:],
            back_values[prefix_length:],
        ],
        1,
    ).astype(bf16)
    back_prefix_kv = jnp.concatenate(
        [back_keys[:prefix_length], back_values[:prefix_length]], 1
    ).astype(bf16)
    grad_attention = jnp.concatenate(
        [jnp.einsum("td,tc->dc", action_norm, back_qkv, preferred_element_type=f32), grad_output], 1
    )
    _, grad_gain_action = norm_back(
        action_rows,
        action_gains[0],
        jnp.einsum(
            "tc,dc->td", back_qkv, attention_full[:, :qkv_width], preferred_element_type=f32
        ),
    )
    grad_prefix = jnp.einsum("td,tc->dc", prefix_norm, back_prefix_kv, preferred_element_type=f32)
    _, grad_gain_prefix = norm_back(
        prefix_rows,
        prefix_gains[0],
        jnp.einsum("tc,dc->td", back_prefix_kv, prefix_full, preferred_element_type=f32),
    )
    grad_prefix_gains, grad_action_gains, grad_readout = lax.psum(
        (
            grad_gain_prefix[None, :],
            jnp.stack([grad_gain_action, grad_gain_hidden, grad_gain_final]),
            grad_readout,
        ),
        ("batch", "wide"),
    )
    terms = (grad_prefix, grad_attention, grad_feedforward)
    shards = (
        lax.psum_scatter(terms[0], "wide", scatter_dimension=0, tiled=True),
        lax.psum_scatter(terms[1], "wide", scatter_dimension=0, tiled=True),
        lax.psum_scatter(terms[2], "wide", scatter_dimension=0, tiled=True),
    )
    shards = lax.psum((shards[0], shards[1], shards[2]), "batch")
    step_rate = learning_rate[0]
    first = advance(
        prefix_weight, prefix_weight_moment, prefix_weight_average, shards[0], step_rate
    )
    second = advance(
        attention_weight, attention_weight_moment, attention_weight_average, shards[1], step_rate
    )
    third = advance(
        feedforward_weight,
        feedforward_weight_moment,
        feedforward_weight_average,
        shards[2],
        step_rate,
    )
    fourth = advance(
        prefix_gains, prefix_gains_moment, prefix_gains_average, grad_prefix_gains, step_rate
    )
    fifth = advance(
        action_gains, action_gains_moment, action_gains_average, grad_action_gains, step_rate
    )
    sixth = advance(
        readout_weight, readout_weight_moment, readout_weight_average, grad_readout, step_rate
    )
    return (
        loss_value,
        first[0],
        second[0],
        third[0],
        fourth[0],
        fifth[0],
        sixth[0],
        first[1],
        second[1],
        third[1],
        fourth[1],
        fifth[1],
        sixth[1],
        first[2],
        second[2],
        third[2],
        fourth[2],
        fifth[2],
        sixth[2],
    )


def solution(mesh):
    return jax.shard_map(
        on_device,
        mesh=mesh,
        in_specs=(
            P(("batch", "wide"), None, None),
            P(("batch", "wide"), None, None),
            P(("batch", "wide"), None, None),
            P(("batch", "wide"), None, None),
            P(("batch", "wide"), None),
            P(("batch", "wide"), None),
            P(("batch", "wide"), None),
            P(),
            P("wide", None),
            P("wide", None),
            P("wide", None, None),
            P(),
            P(),
            P(),
            P("wide", None),
            P("wide", None),
            P("wide", None, None),
            P(),
            P(),
            P(),
            P("wide", None),
            P("wide", None),
            P("wide", None, None),
            P(),
            P(),
            P(),
        ),
        out_specs=(
            P(),
            P("wide", None),
            P("wide", None),
            P("wide", None, None),
            P(),
            P(),
            P(),
            P("wide", None),
            P("wide", None),
            P("wide", None, None),
            P(),
            P(),
            P(),
            P("wide", None),
            P("wide", None),
            P("wide", None, None),
            P(),
            P(),
            P(),
        ),
        check_vma=False,
    )
```

profile of v0, /device:TPU:0, one launch (start us, length us, event | category | flops | bytes accessed | tf_op | source)
XLA Modules:
  0.0 1354.9 jit_solution(13032150080626966623)
XLA Ops:
  15.2 42.5 %psum.57 = f32[]{:T(128)} all-reduce(f32[]{:T(128)} %convert_reduce_fusion), channel_id=1, replica_groups=mesh['batch'=2,'wide'=16] {'batch','wide'}, use_global_device_ids=true, to_apply=%region_11.12 | all-reduce | flops 1 | bytes 8 | tf_op jit(solution)/shard_map/psum | solution.py:144
  62.3 5.6 convolution_convert_fusion
  68.0 70.2 %all-gather.4.cloned.1.call-done = bf16[1024,4608]{1,0:T(8,128)(2,1)} async-done(((bf16[64,4608]{1,0:T(8,128)(2,1)}), bf16[1024,4608]{1,0:T(8,128)(2,1)}) %all-gather.4.cloned.1.call-update) | async-done | bytes 9437200 | tf_op jit(solution)/shard_map/all_gather | solution.py:102
  138.3 4.1 fusion.28
  146.1 3.7 fusion.98
  156.3 4.1 multiply_reduce_fusion.6
  160.6 106.5 %all-gather.8.cloned.1.call-done = bf16[4096,3,1024]{2,0,1:T(8,128)(2,1)} async-done(((bf16[256,3,1024]{2,0,1:T(8,128)(2,1)}), bf16[4096,3,1024]{2,0,1:T(8,128)(2,1)}) %all-gather.8.cloned.1.call-update) | async-done | bytes 25165840 | tf_op jit(solution)/shard_map/all_gather | solution.py:103
  267.1 5.7 fusion.8
  272.9 6.0 multiply_convert_fusion.2
  278.9 6.6 multiply_reduce_fusion.5
  289.5 7.6 multiply_convert_fusion.1
  297.1 7.3 fusion.7
  304.4 6.0 multiply_reduce_fusion.2
  310.8 4.4 fusion.43
  317.7 6.1 fusion.40
  323.8 6.6 multiply_reduce_fusion
  337.2 4.7 fusion.55
  344.1 4.3 multiply_convert_fusion.3
  351.6 7.3 pad_maximum_fusion.1
  358.9 10.1 convolution_bitcast_fusion.1
  369.0 8.2 convolution_bitcast_fusion.2
  377.2 8.3 convolution_bitcast_fusion
  385.5 34.2 %pad_maximum_fusion = f32[4096,3,1024]{2,0,1:T(8,128)} fusion(f32[4096,1,1024]{2,0,1:T(8,128)} %convolution_bitcast_fusion, f32[4096,1,1024]{2,0,1:T(8,128)} %convolution_bitcast_fusion.1, f32[4096,1,1024]{2,0,1:T(8,128)} %convolution_bitcast_fusion.2), kind=kLoop, calls=%fused_computation | loop fusion | flops 25165824 | bytes 100663296 | tf_op jit(solution)/shard_map/stack | solution.py:173
  422.5 190.5 %reduce-scatter.6.cloned.1.call-done = f32[64,4608]{1,0:T(8,128)} async-done(((f32[1024,4608]{1,0:T(8,128)}), f32[64,4608]{1,0:T(8,128)}) %reduce-scatter.6.cloned.1.call-update) | async-done | bytes 1179664 | tf_op jit(solution)/shard_map/reduce_scatter | solution.py:239
  613.0 471.6 %reduce-scatter.8.cloned.1.call-done = f32[256,3,1024]{2,0,1:T(8,128)} async-done(((f32[4096,3,1024]{2,0,1:T(8,128)}), f32[256,3,1024]{2,0,1:T(8,128)}) %reduce-scatter.8.cloned.1.call-update) | async-done | bytes 3145744 | tf_op jit(solution)/shard_map/reduce_scatter | solution.py:240
  1085.4 4.2 fusion.58
  1090.2 4.1 fusion.4
  1094.3 40.1 %all-reduce = (f32[]{:T(128)}, f32[1,2048]{1,0:T(1,128)}, f32[3,1024]{1,0:T(4,128)}) all-reduce(f32[]{:T(128)} %get-tuple-element.64, f32[1,2048]{1,0:T(1,128)} %bitcast.152, f32[3,1024]{1,0:T(4,128)S(1)} %pad_maximum_fusion.8), channel_id=1, replica_groups=mesh['batch'=2,'wide'=16] {'batch','wide'}, use_global_device_ids=true, to_apply=%region_9.10 | all-reduce | flops 5121 | bytes 40968 | tf_op jit(solution)/shard_map/psum | solution.py:144
  1138.5 74.7 %all-reduce.5.cloned.1.call-done = f32[1024,32]{0,1:T(8,128)} async-done(((f32[1024,32]{0,1:T(8,128)}), f32[1024,32]{0,1:T(8,128)}) %all-reduce.5.cloned.1.call-update) | async-done | bytes 131088 | tf_op jit(solution)/shard_map/psum | solution.py:228
  1214.9 117.3 %all-reduce.7.cloned.1.call-done = (f32[128,512]{1,0:T(8,128)}, f32[64,4608]{1,0:T(8,128)}, f32[256,3,1024]{2,0,1:T(8,128)}) async-done(((f32[128,512]{1,0:T(8,128)}, f32[64,4608]{1,0:T(8,128)}, f32[256,3,1024]{2,0,1:T(8,128)}), (f32[128,512]{1,0:T(8,128)}, f32[64,4608]{1,0:T(8,128)}, f32[256,3,1024]{2,0,1:T(8,128)})) %all-reduce.7.cloned.1.call-update) | async-done | bytes 4587536 | tf_op jit(solution)/shard_map/psum | solution.py:242
  1334.3 3.9 multiply_add_fusion.2
  1338.9 7.6 multiply_add_fusion
  (180 shorter events, 52.1 us)
Async XLA Ops:
  7.2 55.1 %all-gather.6.cloned.1.call-start = ((), (), s32[]{:S(2)}) async-start(), calls=%async_computation.4 | async-start | bytes 2228224 | tf_op jit(solution)/shard_map/all_gather | solution.py:101
  8.9 48.8 %copy-start.51 = (s32[1,256]{1,0:T(1,128)S(1)}, s32[1,256]{1,0:T(1,128)}, u32[]{:S(2)}) copy-start(s32[1,256]{1,0:T(1,128)} %param.32) | copy-start | bytes 3076
  8.9 49.3 %copy-start.16 = (bf16[1,256,1024]{2,1,0:T(8,128)(2,1)S(1)}, bf16[1,256,1024]{2,1,0:T(8,128)(2,1)}, u32[]{:S(2)}) copy-start(bf16[1,256,1024]{2,1,0:T(8,128)(2,1)} %param.27) | copy-start | bytes 1572868
  8.9 129.3 %all-gather.4.cloned.1.call-start = ((), (), s32[]{:S(2)}) async-start(), calls=%async_computation.3 | async-start | bytes 10027008 | tf_op jit(solution)/shard_map/all_gather | solution.py:102
  11.2 255.9 %all-gather.8.cloned.1.call-start = ((), (), s32[]{:S(2)}) async-start(), calls=%async_computation.5 | async-start | bytes 26738688 | tf_op jit(solution)/shard_map/all_gather | solution.py:103
  14.5 47.1 %copy-start.44 = (f32[3,1024]{1,0:T(4,128)S(1)}, f32[3,1024]{1,0:T(4,128)}, u32[]{:S(2)}) copy-start(f32[3,1024]{1,0:T(4,128)} %param.38) | copy-start | bytes 36868
  14.5 47.1 %copy-start.47 = (s32[1,256]{1,0:T(1,128)S(1)}, s32[1,256]{1,0:T(1,128)}, u32[]{:S(2)}) copy-start(s32[1,256]{1,0:T(1,128)} %param.31) | copy-start | bytes 3076
  14.5 47.3 %copy-start.48 = (s32[1,1024]{1,0:T(1,128)S(1)}, s32[1,1024]{1,0:T(1,128)}, u32[]{:S(2)}) copy-start(s32[1,1024]{1,0:T(1,128)} %param.30) | copy-start | bytes 12292
  14.5 47.7 %copy-start.46 = (f32[1,2048]{1,0:T(1,128)S(1)}, f32[1,2048]{1,0:T(1,128)}, u32[]{:S(2)}) copy-start(f32[1,2048]{1,0:T(1,128)} %param.37) | copy-start | bytes 24580
  14.6 407.9 %reduce-scatter.4.cloned.1.call-start = ((), (), s32[]{:S(2)}) async-start(), calls=%async_computation.6 | async-start | bytes 4456448 | tf_op jit(solution)/shard_map/reduce_scatter | solution.py:238
  61.6 274.0 %copy-start.49 = (f32[1024]{0:T(1024)}, f32[1024]{0:T(1024)S(1)}, u32[]{:S(2)}) copy-start(f32[1024]{0:T(1024)S(1)} %add_rsqrt_fusion) | copy-start | bytes 12292
  68.0 78.1 %copy-start.38 = (bf16[1024,256]{1,0:T(8,128)(2,1)}, bf16[1024,256]{1,0:T(8,128)(2,1)S(1)}, u32[]{:S(2)}) copy-start(bf16[1024,256]{1,0:T(8,128)(2,1)S(1)} %get-tuple-element.52) | copy-start | bytes 1572868
  68.0 83.5 %copy-start.19 = (bf16[1024,256]{1,0:T(8,128)(2,1)}, bf16[1024,256]{1,0:T(8,128)(2,1)S(1)}, u32[]{:S(2)}) copy-start(bf16[1024,256]{1,0:T(8,128)(2,1)S(1)} %get-tuple-element.51) | copy-start | bytes 1572868
  160.4 118.5 %copy-start.7 = (f32[256,1024]{1,0:T(8,128)}, f32[256,1024]{1,0:T(8,128)S(1)}, u32[]{:S(2)}) copy-start(f32[256,1024]{1,0:T(8,128)S(1)} %get-tuple-element.59) | copy-start | bytes 3145732
  317.7 12.8 slice-start
  317.7 12.8 slice-start.1
  341.9 271.1 %reduce-scatter.6.cloned.1.call-start = ((), (), s32[]{:S(2)}) async-start(), calls=%async_computation.7 | async-start | bytes 20054016 | tf_op jit(solution)/shard_map/reduce_scatter | solution.py:239
  358.9 725.8 %reduce-scatter.8.cloned.1.call-start = ((), (), s32[]{:S(2)}) async-start(), calls=%async_computation.8 | async-start | bytes 53477376 | tf_op jit(solution)/shard_map/reduce_scatter | solution.py:240
  358.9 10.1 copy-start.14
  369.0 8.2 copy-start.12
  419.7 665.6 %copy-start.18 = (bf16[1,256,1024]{2,1,0:T(8,128)(2,1)S(1)}, bf16[1,256,1024]{2,1,0:T(8,128)(2,1)}, u32[]{:S(2)}) copy-start(bf16[1,256,1024]{2,1,0:T(8,128)(2,1)} %param.27) | copy-start | bytes 1572868
  419.7 665.6 %copy-start.28 = (bf16[256,8,256]{0,2,1:T(8,128)(2,1)S(1)}, bf16[256,8,256]{0,2,1:T(8,128)(2,1)}, u32[]{:S(2)}) copy-start(bf16[256,8,256]{0,2,1:T(8,128)(2,1)} %copy-done.27) | copy-start | bytes 3145732
  419.8 793.5 %all-reduce.5.cloned.1.call-start = ((), (), s32[]{:S(2)}) async-start(), calls=%async_computation.9 | async-start | bytes 262144 | tf_op jit(solution)/shard_map/psum | solution.py:228
  422.4 909.8 %all-reduce.7.cloned.1.call-start = ((), (), s32[]{:S(2)}) async-start(), calls=%async_computation.10 | async-start | bytes 9175040 | tf_op jit(solution)/shard_map/psum | solution.py:242
  1090.1 123.1 %copy-start.23 = (f32[1024,32]{0,1:T(8,128)S(1)}, f32[1024,32]{0,1:T(8,128)}, u32[]{:S(2)}) copy-start(f32[1024,32]{0,1:T(8,128)} %param.39) | copy-start | bytes 393220
  1090.1 123.1 %copy-start.41 = (f32[1024,32]{0,1:T(8,128)S(1)}, f32[1024,32]{0,1:T(8,128)}, u32[]{:S(2)}) copy-start(f32[1024,32]{0,1:T(8,128)} %param.51) | copy-start | bytes 393220
  1090.1 123.1 %copy-start.42 = (f32[1024,32]{0,1:T(8,128)S(1)}, f32[1024,32]{0,1:T(8,128)}, u32[]{:S(2)}) copy-start(f32[1024,32]{0,1:T(8,128)} %param.45) | copy-start | bytes 393220
  1090.1 242.1 %copy-start.30 = (f32[128,512]{1,0:T(8,128)S(1)}, f32[128,512]{1,0:T(8,128)}, u32[]{:S(2)}) copy-start(f32[128,512]{1,0:T(8,128)} %param.34) | copy-start | bytes 786436
  1090.1 242.1 %copy-start.39 = (f32[128,512]{1,0:T(8,128)S(1)}, f32[128,512]{1,0:T(8,128)}, u32[]{:S(2)}) copy-start(f32[128,512]{1,0:T(8,128)} %param.46) | copy-start | bytes 786436
  1090.1 242.1 %copy-start.40 = (f32[128,512]{1,0:T(8,128)S(1)}, f32[128,512]{1,0:T(8,128)}, u32[]{:S(2)}) copy-start(f32[128,512]{1,0:T(8,128)} %param.40) | copy-start | bytes 786436
  1090.1 244.1 %copy-start.3 = (f32[64,4608]{1,0:T(8,128)S(1)}, f32[64,4608]{1,0:T(8,128)}, u32[]{:S(2)}) copy-start(f32[64,4608]{1,0:T(8,128)} %param.35) | copy-start | bytes 3538948
  1090.1 244.1 %copy-start.24 = (f32[64,4608]{1,0:T(8,128)S(1)}, f32[64,4608]{1,0:T(8,128)}, u32[]{:S(2)}) copy-start(f32[64,4608]{1,0:T(8,128)} %param.47) | copy-start | bytes 3538948
  (32 other events, 146.0 us)
Sparse Core Ops, SparseCore 0:
  10.8 44.3 all-gather.5
  58.0 80.2 all-gather.3
  140.4 126.6 all-gather.7
  342.1 72.3 reduce-scatter.3
  418.9 194.0 reduce-scatter.5
  617.7 466.8 reduce-scatter.7
  1091.7 121.5 all-reduce.4
  1216.0 116.0 all-reduce.6
where the time goes:
time: 1360 us; the launch traced here: 1350 us
  waiting for transfers between devices  1030 us (76%)
  matrix products  131 us (10%)
  blocking collectives  82.6 us (6%)
  other arithmetic  76.3 us (6%)
  between operations  18.6 us (1%)
  local copies, waits for them, and re-layouts  14.7 us (1%)
    reduce_scatter x1, waiting for transfers between devices, on_device(): lax.psum_scatter(terms[2], 'wide', scatter_dimension=0, tiled=True)  472 us
    reduce_scatter x1, waiting for transfers between devices, on_device(): lax.psum_scatter(terms[1], 'wide', scatter_dimension=0, tiled=True)  191 us
    psum x1, waiting for transfers between devices, on_device(): shards = lax.psum((shards[0], shards[1], shards[2]), 'batch')  117 us
    all_gather x1, waiting for transfers between devices, on_device(): lax.all_gather(masters[2], 'wide', axis=0, tiled=True)  106 us
    psum x2, blocking collectives, on_device(): lax.psum((jnp.sum(valid_rows * error_term * error_term), jnp.sum(valid_ro...  82.6 us
    psum x1, waiting for transfers between devices, on_device(): lax.psum((grad_gain_prefix[None, :], jnp.stack([grad_gain_action, grad_ga...  74.7 us
    all_gather x1, waiting for transfers between devices, on_device(): lax.all_gather(masters[1], 'wide', axis=0, tiled=True)  70.2 us
    another operation x1, other arithmetic, on_device(): jnp.stack([jnp.einsum('tf,td->fd', back_gate, hidden_norm, preferred_elem...  34.2 us
  transfers between devices with their start and end apart: 8, of which 6 were waited for; matrix products, arithmetic and copies ran while one was open for 9% of the time, Pallas kernels for 0%

commit v1 on v0

v1 whole, which is shorter than its diff:
```python
import functools
import math

import jax
import jax.numpy as jnp
from jax import lax
from jax.experimental import pallas as pl
from jax.experimental.pallas import tpu as pltpu
from jax.sharding import PartitionSpec as P

HEADS = 8
HEAD_DIM = 256
QUERY_WIDTH = HEADS * HEAD_DIM
QKV_WIDTH = QUERY_WIDTH + 2 * HEAD_DIM
SCORE_SCALE = HEAD_DIM ** (-0.5)

NORM_EPSILON = 1e-06
MOMENTUM = 0.9
AVERAGE_DECAY = 0.8
NEGATIVE = -1e30

bf16 = jnp.bfloat16
f32 = jnp.float32
HIGHEST = lax.Precision.HIGHEST
VMEM_LIMIT = 48 * 2**20


def rms_norm(stream, gain_row):
    return (
        stream
        * lax.rsqrt(jnp.mean(stream * stream, axis=-1, keepdims=True) + NORM_EPSILON)
        * (1.0 + gain_row)
    )


def norm_back(stream, gain_row, cotangent):
    _, pull = jax.vjp(rms_norm, stream, gain_row)
    return pull(cotangent)


def gated_unit(gate_value, linear_value):
    return jax.nn.gelu(gate_value, approximate=True) * linear_value


def visible(prefix_ids, action_ids, block_flags):
    length = block_flags.shape[0]
    place = jnp.arange(length)
    upto = place[None, :] <= place[:, None]
    levels = jnp.sum(jnp.where(upto, block_flags[None, :], 0), axis=1)
    from_prefix = prefix_ids[:, None] == action_ids[None, :]
    from_action = (action_ids[:, None] == action_ids[None, :]) & (
        levels[:, None] <= levels[None, :]
    )
    return jnp.concatenate([from_prefix, from_action], axis=0).astype(jnp.int32)


def advance(weight, moment, average, gradient, step_rate):
    moment_next = MOMENTUM * moment + gradient
    weight_next = weight - step_rate * (gradient + MOMENTUM * moment_next)
    average_next = AVERAGE_DECAY * average + (1.0 - AVERAGE_DECAY) * weight_next
    return (weight_next, moment_next, average_next)


def mm(a, b, contract, out=f32):
    return lax.dot_general(
        a, b, (((contract[0],), (contract[1],)), ((), ())), preferred_element_type=f32
    ).astype(out)


class Ring:
    def __init__(self, wide):
        chips = wide // 2
        self.wide, self.chips = wide, chips
        self.cycle = list(range(0, chips, 2)) + list(range(1, chips, 2))[::-1]
        ahead = [(self.cycle[i], self.cycle[(i + 1) % chips]) for i in range(chips)]
        self.right = [(2 * s + c, 2 * t + c) for s, t in ahead for c in (0, 1)]
        self.left = [(t, s) for s, t in self.right]
        self.core = [(w, w ^ 1) for w in range(wide)]
        self.n_right = chips // 2
        self.n_left = chips - 1 - self.n_right

    def to_right(self, v):
        return lax.ppermute(v, "wide", self.right)

    def to_left(self, v):
        return lax.ppermute(v, "wide", self.left)

    def to_core(self, v):
        return lax.ppermute(v, "wide", self.core)

    def to_peer(self, v):
        return lax.ppermute(v, "batch", [(0, 1), (1, 0)])

    def owners(self):
        chip = lax.axis_index("wide") // 2
        place = [self.cycle.index(i) for i in range(self.chips)]
        here = jnp.array(place, jnp.int32)[chip]
        cycle = jnp.array(self.cycle, jnp.int32)
        rights = [cycle[(here - d + self.chips) % self.chips] for d in range(1, self.n_right + 1)]
        lefts = [cycle[(here + d) % self.chips] for d in range(1, self.n_left + 1)]
        return chip, rights, lefts

    def gather(self, shard, axis):
        half = shard.shape[axis] // 2
        me = lax.axis_index("batch")
        right, left = [], []
        if half % 16:
            r = l = shard
            for d in range(self.n_right):
                r = self.to_right(r)
                right.append((r,))
                if d < self.n_left:
                    l = self.to_left(l)
                    left.append(l)
            return right, left
        r = lax.dynamic_slice_in_dim(shard, me * half, half, axis)
        l = shard
        for d in range(self.n_right):
            r = self.to_right(r)
            if d < self.n_left:
                l = self.to_left(l)
                left.append(l)
            right.append((r, self.to_peer(r)))
        return right, left

    def scatter(self, own, right, left, axis):
        def add(u, v):
            return (u.astype(f32) + v.astype(f32)).astype(bf16)

        half = own.shape[axis] // 2
        me = lax.axis_index("batch")
        r = l = None
        split = half % 16 == 0
        for d in range(self.n_right - 1, -1, -1):
            mine = add(right[d][0], self.to_peer(right[d][1])) if split else right[d][0]
            r = self.to_left(mine if r is None else add(mine, r))
            if d < self.n_left:
                l = self.to_right(left[d] if l is None else add(left[d], l))
        whole = add(own, l)
        if not split:
            whole = add(whole, r)
            return whole.astype(f32) + self.to_peer(whole).astype(f32)
        mine = lax.dynamic_slice_in_dim(whole, me * half, half, axis)
        other = lax.dynamic_slice_in_dim(whole, (1 - me) * half, half, axis)
        total = (mine.astype(f32) + r.astype(f32) + self.to_peer(other).astype(f32)).astype(bf16)
        across = self.to_peer(total)
        return jnp.where(
            me == 0,
            jnp.concatenate([total, across], axis),
            jnp.concatenate([across, total], axis),
        ).astype(f32)

    def sum_all(self, v):
        k = 1
        while k < self.wide:
            v = v + lax.ppermute(v, "wide", [(w, w ^ k) for w in range(self.wide)])
            k *= 2
        return v + self.to_peer(v)


def assemble(ring, own, right, left, core_own, core_right, core_left, rows_a, width_a):
    half = rows_a // 2
    chip, rights, lefts = ring.owners()
    me, core = lax.axis_index("batch"), lax.axis_index("wide") % 2
    pieces, starts, sizes = [], [], []
    for which, o, rr, ll in ((core, own, right, left), (1 - core, core_own, core_right, core_left)):
        pieces.append(o)
        starts.append((chip * 2 + which, 0))
        sizes.append(rows_a)
        for d, parts in enumerate(rr):
            pieces += list(parts)
            spots = (me * half, (1 - me) * half) if len(parts) == 2 else (0,)
            starts += [(rights[d] * 2 + which, spot) for spot in spots]
            sizes += [p.shape[0] for p in parts]
        for d, whole in enumerate(ll):
            pieces.append(whole)
            starts.append((lefts[d] * 2 + which, 0))
            sizes.append(rows_a)
    n = len(pieces)
    table = jnp.stack([jnp.stack([jnp.asarray(s, jnp.int32) for s, _ in starts]),
                       jnp.stack([jnp.asarray(t, jnp.int32) for _, t in starts])])
    width_p = pieces[0].shape[1] - width_a
    pw = width_p // 2

    def kernel(table_ref, *refs):
        ins, (qkv, out, pre, sems) = refs[:n], refs[n:]
        copies = []
        for i in range(n):
            shard, inner = table_ref[0, i], table_ref[1, i]
            at = pl.multiple_of(shard * rows_a + inner, sizes[i])
            size = sizes[i]
            copies.append((ins[i].at[:, pl.ds(0, QKV_WIDTH)], qkv.at[pl.ds(at, size), :]))
            copies.append((ins[i].at[:, pl.ds(QKV_WIDTH, width_a - QKV_WIDTH)], out.at[pl.ds(at, size), :]))
            for j in (0, 1):
                to = pl.multiple_of(shard * (2 * rows_a) + j * rows_a + inner, sizes[i])
                copies.append((ins[i].at[:, pl.ds(width_a + j * pw, pw)], pre.at[pl.ds(to, size), :]))
        made = [pltpu.make_async_copy(s, t, sems.at[k]) for k, (s, t) in enumerate(copies)]
        for c in made:
            c.start()
        for c in made:
            c.wait()

    total = rows_a * ring.wide
    shapes = ((total, QKV_WIDTH), (total, width_a - QKV_WIDTH), (2 * total, pw))
    return pl.pallas_call(
        kernel,
        out_shape=[jax.ShapeDtypeStruct(sh, bf16) for sh in shapes],
        grid_spec=pltpu.PrefetchScalarGridSpec(
            num_scalar_prefetch=1,
            grid=(1,),
            in_specs=[pl.BlockSpec(memory_space=pl.ANY)] * n,
            out_specs=[pl.BlockSpec(sh, lambda i, t: (0, 0)) for sh in shapes],
            scratch_shapes=[pltpu.SemaphoreType.DMA((4 * n,))],
        ),
        compiler_params=pltpu.CompilerParams(vmem_limit_bytes=VMEM_LIMIT),
        cost_estimate=pl.CostEstimate(
            flops=0, transcendentals=0, bytes_accessed=2 * 2 * total * (width_a + width_p)
        ),
        name="assemble",
    )(table, *pieces)


def gelu_parts(v):
    c = math.sqrt(2.0 / math.pi)
    square = v * v
    t = jnp.tanh(c * v * (1.0 + 0.044715 * square))
    half = 0.5 * (1.0 + t)
    slope = half + 0.5 * v * (1.0 - t * t) * c * (1.0 + 3.0 * 0.044715 * square)
    return v * half, slope


def load_block(refs, buf, sems, k):
    at, made = 0, []
    for j, r in enumerate(refs):
        size = r.shape[1]
        made.append(pltpu.make_async_copy(r, buf.at[:, pl.ds(at, size), :], sems.at[k, j]))
        at += size
    return made


def ff_forward(norm_two, blocks, before):
    nb = len(blocks)
    flat = [a for blk in blocks for a in blk]
    tokens, dim = norm_two.shape
    units = sum(a.shape[1] for a in blocks[0])
    half = tokens // 2
    has_before = before is not None

    def kernel(norm_ref, *refs):
        refs = list(refs)
        ins = [[refs.pop(0) for _ in blk] for blk in blocks]
        if has_before:
            own_in, oth_in = refs.pop(0), refs.pop(0)
        gate_out, lin_out, hid_out, own_out, oth_out, buf, sems = refs
        i = pl.program_id(0)

        @pl.when(i == 0)
        def _():
            for k in range(nb):
                for c in load_block(ins[k], buf.at[k], sems, k):
                    c.start()
            if has_before:
                own_out[...] = own_in[...]
                oth_out[...] = oth_in[...]
            else:
                own_out[...] = jnp.zeros_like(own_out)
                oth_out[...] = jnp.zeros_like(oth_out)

        for k in range(nb):

            @pl.when(i == k)
            def _(k=k):
                for c in load_block(ins[k], buf.at[k], sems, k):
                    c.wait()

        w = buf.at[i]
        gate = mm(norm_ref[...], w[0], (1, 1))
        linear = mm(norm_ref[...], w[1], (1, 1))
        gate_out[0] = gate
        lin_out[0] = linear
        hidden = (gelu_parts(gate)[0] * linear).astype(bf16)
        hid_out[0] = hidden
        own_out[...] += mm(hidden[:half], w[2], (1, 0))
        oth_out[...] += mm(hidden[half:], w[2], (1, 0))

    once = pl.BlockSpec((tokens, dim), lambda i: (0, 0))
    row = pl.BlockSpec((half, dim), lambda i: (0, 0))
    step = pl.BlockSpec((1, tokens, units), lambda i: (i, 0, 0))
    any_space = pl.BlockSpec(memory_space=pl.ANY)
    return pl.pallas_call(
        kernel,
        out_shape=[
            jax.ShapeDtypeStruct((nb, tokens, units), f32),
            jax.ShapeDtypeStruct((nb, tokens, units), f32),
            jax.ShapeDtypeStruct((nb, tokens, units), bf16),
            jax.ShapeDtypeStruct((half, dim), f32),
            jax.ShapeDtypeStruct((half, dim), f32),
        ],
        grid=(nb,),
        in_specs=[once] + [any_space] * len(flat) + [row, row] * has_before,
        out_specs=[step, step, step, row, row],
        scratch_shapes=[
            pltpu.VMEM((nb, 3, units, dim), bf16),
            pltpu.SemaphoreType.DMA((nb, 2)),
        ],
        compiler_params=pltpu.CompilerParams(vmem_limit_bytes=VMEM_LIMIT),
        cost_estimate=pl.CostEstimate(
            flops=6 * nb * tokens * units * dim,
            transcendentals=nb * tokens * units,
            bytes_accessed=nb * (6 * units * dim + 10 * tokens * units),
        ),
        name="ff_forward",
    )(norm_two, *flat, *(before or ()))


def ff_backward(norm_two, branch_two, blocks, kept, picks, before):
    nb = len(blocks)
    flat = [a for blk in blocks for a in blk]
    gate_all, lin_all, hid_all = kept
    tokens, dim = norm_two.shape
    units = sum(a.shape[1] for a in blocks[0])
    half = tokens // 2
    has_before = before is not None
    first, stride = picks

    def kernel(norm_ref, branch_ref, gate_ref, lin_ref, hid_ref, *refs):
        refs = list(refs)
        ins = [[refs.pop(0) for _ in blk] for blk in blocks]
        if has_before:
            own_in, oth_in = refs.pop(0), refs.pop(0)
        outs = [[refs.pop(0) for _ in blk] for blk in blocks]
        own_out, oth_out, buf, grads, sems, out_sems = refs
        i = pl.program_id(0)

        def stores(k):
            at, made = 0, []
            for j, r in enumerate(outs[k]):
                size = r.shape[1]
                made.append(pltpu.make_async_copy(grads.at[k, :, pl.ds(at, size), :], r, out_sems.at[k, j]))
                at += size
            return made

        @pl.when(i == 0)
        def _():
            for k in range(nb):
                for c in load_block(ins[k], buf.at[k], sems, k):
                    c.start()
            if has_before:
                own_out[...] = own_in[...]
                oth_out[...] = oth_in[...]
            else:
                own_out[...] = jnp.zeros_like(own_out)
                oth_out[...] = jnp.zeros_like(oth_out)

        for k in range(nb):

            @pl.when(i == k)
            def _(k=k):
                for c in load_block(ins[k], buf.at[k], sems, k):
                    c.wait()

        w, g = buf.at[i], grads.at[i]
        back_hidden = mm(branch_ref[...], w[2], (1, 1))
        value, slope = gelu_parts(gate_ref[0])
        back_gate = (back_hidden * lin_ref[0] * slope).astype(bf16)
        back_linear = (back_hidden * value).astype(bf16)
        g[0] = mm(back_gate, norm_ref[...], (0, 0), bf16)
        g[1] = mm(back_linear, norm_ref[...], (0, 0), bf16)
        g[2] = mm(hid_ref[0], branch_ref[...], (0, 0), bf16)
        own_out[...] += mm(back_gate[:half], w[0], (1, 0)) + mm(back_linear[:half], w[1], (1, 0))
        oth_out[...] += mm(back_gate[half:], w[0], (1, 0)) + mm(back_linear[half:], w[1], (1, 0))

        for k in range(nb):

            @pl.when(i == k)
            def _(k=k):
                for c in stores(k):
                    c.start()

        @pl.when(i == nb - 1)
        def _():
            for k in range(nb):
                for c in stores(k):
                    c.wait()

    once = pl.BlockSpec((tokens, dim), lambda i: (0, 0))
    row = pl.BlockSpec((half, dim), lambda i: (0, 0))
    step = pl.BlockSpec((1, tokens, units), lambda i: (first + stride * i, 0, 0))
    any_space = pl.BlockSpec(memory_space=pl.ANY)
    made = pl.pallas_call(
        kernel,
        out_shape=[jax.ShapeDtypeStruct(a.shape, bf16) for a in flat]
        + [jax.ShapeDtypeStruct((half, dim), f32)] * 2,
        grid=(nb,),
        in_specs=[once, once, step, step, step] + [any_space] * len(flat) + [row, row] * has_before,
        out_specs=[any_space] * len(flat) + [row, row],
        scratch_shapes=[
            pltpu.VMEM((nb, 3, units, dim), bf16),
            pltpu.VMEM((nb, 3, units, dim), bf16),
            pltpu.SemaphoreType.DMA((nb, 2)),
            pltpu.SemaphoreType.DMA((nb, 2)),
        ],
        compiler_params=pltpu.CompilerParams(vmem_limit_bytes=VMEM_LIMIT),
        cost_estimate=pl.CostEstimate(
            flops=12 * nb * tokens * units * dim,
            transcendentals=nb * tokens * units,
            bytes_accessed=nb * (12 * units * dim + 10 * tokens * units),
        ),
        name="ff_backward",
    )(norm_two, branch_two, gate_all, lin_all, hid_all, *flat, *(before or ()))
    made = list(made)
    grads = [tuple(made.pop(0) for _ in blk) for blk in blocks]
    return grads, made


def attention(action_qkv, prefix_kv, allowed):
    tokens, keys = action_qkv.shape[0], allowed.shape[0]
    n_pre = prefix_kv.shape[0]

    def kernel(q_ref, kv_ref, pre_ref, allowed_ref, out_ref, k_all, v_turned):
        @pl.when(pl.program_id(0) == 0)
        def _():
            k_all[:n_pre] = pre_ref[:, :HEAD_DIM]
            k_all[n_pre:] = kv_ref[:, :HEAD_DIM]
            v_turned[:, :n_pre] = pre_ref[:, HEAD_DIM:].T
            v_turned[:, n_pre:] = kv_ref[:, HEAD_DIM:].T

        scores = mm(k_all[...], q_ref[...], (1, 1)) * SCORE_SCALE
        scores = jnp.where(allowed_ref[...] != 0, scores, NEGATIVE)
        exp_scores = jnp.exp(scores - jnp.max(scores, axis=0, keepdims=True))
        soft = exp_scores / jnp.sum(exp_scores, axis=0, keepdims=True)
        out_ref[...] = mm(v_turned[...], soft.astype(bf16), (1, 0)).T.astype(bf16)

    return pl.pallas_call(
        kernel,
        out_shape=jax.ShapeDtypeStruct((tokens, QUERY_WIDTH), bf16),
        grid=(HEADS,),
        in_specs=[
            pl.BlockSpec((tokens, HEAD_DIM), lambda h: (0, h)),
            pl.BlockSpec((tokens, 2 * HEAD_DIM), lambda h: (0, HEADS // 2)),
            pl.BlockSpec((n_pre, 2 * HEAD_DIM), lambda h: (0, 0)),
            pl.BlockSpec((keys, tokens), lambda h: (0, 0)),
        ],
        out_specs=pl.BlockSpec((tokens, HEAD_DIM), lambda h: (0, h)),
        scratch_shapes=[pltpu.VMEM((keys, HEAD_DIM), bf16), pltpu.VMEM((HEAD_DIM, keys), bf16)],
        compiler_params=pltpu.CompilerParams(vmem_limit_bytes=VMEM_LIMIT),
        cost_estimate=pl.CostEstimate(
            flops=4 * tokens * keys * QUERY_WIDTH,
            transcendentals=HEADS * tokens * keys,
            bytes_accessed=4 * tokens * QUERY_WIDTH + 4 * keys * HEAD_DIM + 4 * keys * tokens,
        ),
        name="attention",
    )(action_qkv, action_qkv, prefix_kv, allowed)


def attention_back(action_qkv, prefix_kv, allowed, back_mixed):
    tokens, keys = action_qkv.shape[0], allowed.shape[0]
    n_pre = prefix_kv.shape[0]

    def kernel(q_ref, kv_ref, pre_ref, allowed_ref, back_ref, qkv_out, pre_out, k_all, v_all, k_turned, k_sum, v_sum):
        h = pl.program_id(0)

        @pl.when(h == 0)
        def _():
            k_all[:n_pre] = pre_ref[:, :HEAD_DIM]
            k_all[n_pre:] = kv_ref[:, :HEAD_DIM]
            v_all[:n_pre] = pre_ref[:, HEAD_DIM:]
            v_all[n_pre:] = kv_ref[:, HEAD_DIM:]
            k_turned[...] = k_all[...].T
            k_sum[...] = jnp.zeros_like(k_sum)
            v_sum[...] = jnp.zeros_like(v_sum)

        query, back = q_ref[...], back_ref[...]
        scores = mm(k_all[...], query, (1, 1)) * SCORE_SCALE
        scores = jnp.where(allowed_ref[...] != 0, scores, NEGATIVE)
        exp_scores = jnp.exp(scores - jnp.max(scores, axis=0, keepdims=True))
        soft = exp_scores / jnp.sum(exp_scores, axis=0, keepdims=True)
        v_sum[...] += mm(soft.astype(bf16), back, (1, 0))
        back_soft = mm(v_all[...], back, (1, 1))
        mean = jnp.sum(soft * back_soft, axis=0, keepdims=True)
        back_scores = (soft * (back_soft - mean)).astype(bf16)
        k_sum[...] += mm(back_scores, query, (1, 0))
        turned = mm(k_turned[...], back_scores, (1, 0)) * SCORE_SCALE
        qkv_out[:, pl.ds(pl.multiple_of(h * HEAD_DIM, HEAD_DIM), HEAD_DIM)] = turned.T.astype(bf16)

        @pl.when(h == HEADS - 1)
        def _():
            pre_out[:, :HEAD_DIM] = (k_sum[:n_pre] * SCORE_SCALE).astype(bf16)
            pre_out[:, HEAD_DIM:] = v_sum[:n_pre].astype(bf16)
            qkv_out[:, QUERY_WIDTH : QUERY_WIDTH + HEAD_DIM] = (k_sum[n_pre:] * SCORE_SCALE).astype(bf16)
            qkv_out[:, QUERY_WIDTH + HEAD_DIM :] = v_sum[n_pre:].astype(bf16)

    return pl.pallas_call(
        kernel,
        out_shape=[
            jax.ShapeDtypeStruct((tokens, QKV_WIDTH), bf16),
            jax.ShapeDtypeStruct((n_pre, 2 * HEAD_DIM), bf16),
        ],
        grid=(HEADS,),
        in_specs=[
            pl.BlockSpec((tokens, HEAD_DIM), lambda h: (0, h)),
            pl.BlockSpec((tokens, 2 * HEAD_DIM), lambda h: (0, HEADS // 2)),
            pl.BlockSpec((n_pre, 2 * HEAD_DIM), lambda h: (0, 0)),
            pl.BlockSpec((keys, tokens), lambda h: (0, 0)),
            pl.BlockSpec((tokens, HEAD_DIM), lambda h: (0, h)),
        ],
        out_specs=[
            pl.BlockSpec((tokens, QKV_WIDTH), lambda h: (0, 0)),
            pl.BlockSpec((n_pre, 2 * HEAD_DIM), lambda h: (0, 0)),
        ],
        scratch_shapes=[
            pltpu.VMEM((keys, HEAD_DIM), bf16),
            pltpu.VMEM((keys, HEAD_DIM), bf16),
            pltpu.VMEM((HEAD_DIM, keys), bf16),
            pltpu.VMEM((keys, HEAD_DIM), f32),
            pltpu.VMEM((keys, HEAD_DIM), f32),
        ],
        compiler_params=pltpu.CompilerParams(vmem_limit_bytes=VMEM_LIMIT),
        cost_estimate=pl.CostEstimate(
            flops=10 * tokens * keys * QUERY_WIDTH,
            transcendentals=HEADS * tokens * keys,
            bytes_accessed=8 * tokens * QUERY_WIDTH + 8 * keys * HEAD_DIM + 4 * keys * tokens,
        ),
        name="attention_back",
    )(action_qkv, action_qkv, prefix_kv, allowed, back_mixed)


def on_device(
    ring,
    prefix_in,
    action_in,
    target,
    valid_mask,
    prefix_ids,
    action_ids,
    action_blocks,
    learning_rate,
    prefix_weight,
    attention_weight,
    feedforward_weight,
    prefix_gains,
    action_gains,
    readout_weight,
    prefix_weight_moment,
    attention_weight_moment,
    feedforward_weight_moment,
    prefix_gains_moment,
    action_gains_moment,
    readout_weight_moment,
    prefix_weight_average,
    attention_weight_average,
    feedforward_weight_average,
    prefix_gains_average,
    action_gains_average,
    readout_weight_average,
):
    core = lax.axis_index("wide") % 2
    rows_a, width_a = attention_weight.shape
    width_p = prefix_weight.shape[1]
    n_right, n_left = ring.n_right, ring.n_left

    prefix_bf = prefix_weight.astype(bf16)
    packed = jnp.concatenate(
        [attention_weight.astype(bf16), prefix_bf[:rows_a], prefix_bf[rows_a:]], axis=1
    )
    a_right, a_left = ring.gather(packed, 0)
    swap = ring.to_core
    qkv_weight, output_weight, prefix_full = assemble(
        ring,
        packed,
        a_right,
        a_left,
        swap(packed),
        [tuple(swap(u) for u in parts) for parts in a_right],
        [swap(u) for u in a_left],
        rows_a,
        width_a,
    )
    ff_own = jnp.transpose(feedforward_weight, (1, 0, 2)).astype(bf16)
    f_right, f_left = ring.gather(ff_own, 1)
    own = [("own", 0)]
    order = own + [x for d in range(n_right) for x in ([("left", d)] if d < n_left else []) + [("right", d)]]
    weights = {("own", 0): (ff_own,)}
    weights.update({("left", d): (w,) for d, w in enumerate(f_left)})
    weights.update({("right", d): pair for d, pair in enumerate(f_right)})
    groups = [order[: 1 + 2 * (n_left - 1)], order[1 + 2 * (n_left - 1) :]]

    prefix_rows = prefix_in[0].astype(f32)
    action_rows = action_in[0].astype(f32)
    target_rows = target[0]
    valid_rows = valid_mask[0].astype(f32)
    allowed = visible(prefix_ids[0], action_ids[0], action_blocks[0])
    prefix_norm = rms_norm(prefix_rows, prefix_gains[0]).astype(bf16)
    action_norm = rms_norm(action_rows, action_gains[0]).astype(bf16)
    prefix_kv = mm(prefix_norm, prefix_full, (1, 0), bf16)
    action_qkv = mm(action_norm, qkv_weight, (1, 0), bf16)
    mixed_heads = attention(action_qkv, prefix_kv, allowed)
    residual = action_rows + mm(mixed_heads, output_weight, (1, 1))
    tokens = residual.shape[0]
    hidden_norm = rms_norm(residual, action_gains[1]).astype(bf16)
    norm_two = jnp.concatenate([hidden_norm, swap(hidden_norm)], 0)
    kept, branch = [], None
    for group in groups:
        *values, own_rows, other_rows = ff_forward(norm_two, [weights[x] for x in group], branch)
        kept.append(values)
        branch = (own_rows, other_rows)
    final_stream = residual + branch[0] + swap(branch[1])
    final_norm = rms_norm(final_stream, action_gains[2])
    predicted = jnp.dot(final_norm, readout_weight, precision=HIGHEST)
    error_term = predicted - target_rows

    loss_sum = jnp.sum(valid_rows * error_term * error_term)
    own_count = jnp.sum(valid_rows)
    back_predicted = 2.0 * valid_rows * error_term
    grad_readout = lax.dot_general(
        back_predicted, final_norm, (((0,), (0,)), ((), ())), precision=HIGHEST
    )
    back_final, grad_gain_final = norm_back(
        final_stream, action_gains[2], jnp.dot(back_predicted, readout_weight.T, precision=HIGHEST)
    )
    back_branch = back_final.astype(bf16)
    branch_two = jnp.concatenate([back_branch, swap(back_branch)], 0)
    back, grads = None, {}
    for group, values in zip(reversed(groups), reversed(kept)):
        last = len(group) - 1
        made, back = ff_backward(
            norm_two, branch_two, [weights[x] for x in group[::-1]], values, (last, -1), back
        )
        grads.update(zip(group[::-1], made))
    ff_sum = ring.scatter(
        grads["own", 0][0],
        [grads["right", d] for d in range(n_right)],
        [grads["left", d][0] for d in range(n_left)],
        1,
    )
    back_norm_in = back[0] + swap(back[1])
    back_norm_out, grad_gain_hidden = norm_back(residual, action_gains[1], back_norm_in)
    back_residual = back_final + back_norm_out
    back_attention = back_residual.astype(bf16)
    back_mixed = mm(back_attention, output_weight, (1, 0), bf16)
    back_qkv, back_prefix_kv = attention_back(action_qkv, prefix_kv, allowed, back_mixed)

    def by_core(v, size):
        cut = v.reshape(v.shape[0], ring.chips, 2, size)
        cut = jnp.transpose(cut, (2, 0, 1, 3)).reshape(2, v.shape[0], ring.chips * size)
        return (
            lax.dynamic_index_in_dim(cut, core, 0, False),
            lax.dynamic_index_in_dim(cut, 1 - core, 0, False),
        )

    norm_mine, norm_other = by_core(action_norm, rows_a)
    attn_mine, attn_other = by_core(back_attention, rows_a)
    norm_rows = jnp.concatenate([norm_mine, swap(norm_other)], 0)
    attn_rows = jnp.concatenate([attn_mine, swap(attn_other)], 0)
    qkv_rows = jnp.concatenate([back_qkv, swap(back_qkv)], 0)
    mixed_rows = jnp.concatenate([mixed_heads, swap(mixed_heads)], 0)
    grad_qkv = mm(norm_rows, qkv_rows, (0, 0), bf16)
    grad_output = mm(attn_rows, mixed_rows, (0, 0), bf16)
    grad_prefix = mm(prefix_norm, back_prefix_kv, (0, 0), bf16)
    grad_prefix = grad_prefix.reshape(ring.chips, 2, 2, rows_a, width_p).transpose(1, 0, 3, 2, 4)
    grad_prefix = grad_prefix.reshape(2, ring.chips * rows_a, 2 * width_p)
    prefix_mine = lax.dynamic_index_in_dim(grad_prefix, core, 0, False)
    prefix_other = lax.dynamic_index_in_dim(grad_prefix, 1 - core, 0, False)
    prefix_sum = (prefix_mine.astype(f32) + swap(prefix_other).astype(f32)).astype(bf16)
    grad_packed = jnp.concatenate([grad_qkv, grad_output, prefix_sum], 1)
    chip, rights, lefts = ring.owners()
    me, cut = lax.axis_index("batch"), rows_a // 2

    def rows_of(owner, start, size):
        return lax.dynamic_slice_in_dim(grad_packed, owner * rows_a + start, size, 0)

    packed_sum = ring.scatter(
        rows_of(chip, 0, rows_a),
        [
            (rows_of(o, me * cut, cut), rows_of(o, (1 - me) * cut, cut))
            if len(parts) == 2
            else (rows_of(o, 0, rows_a),)
            for o, parts in zip(rights, a_right)
        ],
        [rows_of(o, 0, rows_a) for o in lefts],
        0,
    )

    _, grad_gain_action = norm_back(
        action_rows, action_gains[0], mm(back_qkv, qkv_weight, (1, 1))
    )
    _, grad_gain_prefix = norm_back(
        prefix_rows, prefix_gains[0], mm(back_prefix_kv, prefix_full, (1, 1))
    )
    dim = action_rows.shape[1]
    small = jnp.concatenate(
        [
            grad_readout,
            grad_gain_prefix.reshape(-1, dim),
            grad_gain_action[None],
            grad_gain_hidden[None],
            grad_gain_final[None],
            jnp.full((1, dim), loss_sum),
            jnp.full((1, dim), own_count),
        ],
        0,
    )
    small = ring.sum_all(small)
    act = grad_readout.shape[0]
    n_pre = grad_gain_prefix.shape[0] // dim
    count = small[act + n_pre + 4, 0]
    loss_value = small[act + n_pre + 3, 0] / count
    scale = 1.0 / count
    step_rate = learning_rate[0]
    first = advance(
        prefix_weight,
        prefix_weight_moment,
        prefix_weight_average,
        jnp.concatenate(
            [packed_sum[:, width_a : width_a + width_p], packed_sum[:, width_a + width_p :]], 0
        )
        * scale,
        step_rate,
    )
    second = advance(
        attention_weight,
        attention_weight_moment,
        attention_weight_average,
        packed_sum[:, :width_a] * scale,
        step_rate,
    )
    third = advance(
        feedforward_weight,
        feedforward_weight_moment,
        feedforward_weight_average,
        jnp.transpose(ff_sum, (1, 0, 2)) * scale,
        step_rate,
    )
    fourth = advance(
        prefix_gains,
        prefix_gains_moment,
        prefix_gains_average,
        small[act : act + n_pre].reshape(1, -1) * scale,
        step_rate,
    )
    fifth = advance(
        action_gains,
        action_gains_moment,
        action_gains_average,
        small[act + n_pre : act + n_pre + 3] * scale,
        step_rate,
    )
    sixth = advance(
        readout_weight,
        readout_weight_moment,
        readout_weight_average,
        small[:act].T * scale,
        step_rate,
    )
    return (loss_value,) + tuple(
        group[i]
        for i in range(3)
        for group in (first, second, third, fourth, fifth, sixth)
    )


def solution(mesh):
    rows = P(("batch", "wide"))
    wide = P("wide")
    whole = P()
    weights = (wide, wide, wide, whole, whole, whole)
    return jax.shard_map(
        functools.partial(on_device, Ring(mesh.shape["wide"])),
        mesh=mesh,
        in_specs=(rows,) * 7 + (whole,) + weights * 3,
        out_specs=(whole,) + weights * 3,
        check_vma=False,
    )
```

time: 1360 us -> 617 us (0.45)
  waiting for transfers between devices: 1030 us -> 302 us
  matrix products: 131 us -> 33.7 us
  Pallas kernels: 0 us -> 93.1 us
  blocking collectives: 82.6 us -> 0 us
  starting transfers between devices: 0.79 us -> 74.7 us
  other arithmetic: 76.3 us -> 44.2 us
  local copies, waits for them, and re-layouts: 14.7 us -> 43.1 us
    reduce_scatter x3 -> x0, waiting for transfers between devices: 662 us -> none  [the longest x1 472 us: on_device(): lax.psum_scatter(terms[2], 'wide', scatter_dimension=0, tiled=True)]
    ppermute x0 -> x74, waiting for transfers between devices: none -> 302 us  [the longest x14 118 us: to_right(): return lax.ppermute(v, 'wide', self.right)]
    psum x2 -> x0, waiting for transfers between devices: 192 us -> none  [the longest x1 117 us: on_device(): shards = lax.psum((shards[0], shards[1], shards[2]), 'batch')]
    all_gather x3 -> x0, waiting for transfers between devices: 177 us -> none  [the longest x1 106 us: on_device(): lax.all_gather(masters[2], 'wide', axis=0, tiled=True)]
    dot_general x27 -> x12, matrix products: 131 us -> 33.7 us  [the longest x9 27.9 us: mm(): lax.dot_general(a, b, (((contract[0],), (contract[1],)), ((), ())), prefe...]
    pallas_call x0 -> x7, Pallas kernels: none -> 93.1 us  [the longest x2 34.3 us: ff_backward(): pl.pallas_call(kernel, out_shape=[jax.ShapeDtypeStruct(a.shape, bf16) for...]
    psum x2 -> x0, blocking collectives: 82.6 us -> none  [on_device(): lax.psum((jnp.sum(valid_rows * error_term * error_term), jnp.sum(valid_ro...]
    ppermute x0 -> x74, starting transfers between devices: none -> 74.7 us  [the longest x21 29.7 us: to_peer(): return lax.ppermute(v, 'batch', [(0, 1), (1, 0)])]
  transfers between devices with their start and end apart: 8 -> 74, of which waited for: 6 -> 30; matrix products, arithmetic and copies ran while one was open for 9% -> 15% of each run, Pallas kernels for 0% -> 8%
where the time goes in v1:
time: 617 us; the launch traced here: 611 us
  waiting for transfers between devices  302 us (49%)
  Pallas kernels  93.1 us (15%)
  starting transfers between devices  74.7 us (12%)
  other arithmetic  44.2 us (7%)
  local copies, waits for them, and re-layouts  43.1 us (7%)
  matrix products  33.7 us (5%)
  between operations  20 us (3%)
    ppermute x14, waiting for transfers between devices, to_right(): return lax.ppermute(v, 'wide', self.right)  118 us
    ppermute x21, waiting for transfers between devices, to_peer(): return lax.ppermute(v, 'batch', [(0, 1), (1, 0)])  115 us
    ppermute x14, waiting for transfers between devices, to_left(): return lax.ppermute(v, 'wide', self.left)  54.4 us
    pallas_call x2, Pallas kernels, ff_backward(): pl.pallas_call(kernel, out_shape=[jax.ShapeDtypeStruct(a.shape, bf16) for...  34.3 us
    ppermute x21, starting transfers between devices, to_peer(): return lax.ppermute(v, 'batch', [(0, 1), (1, 0)])  29.7 us
    dot_general x9, matrix products, mm(): lax.dot_general(a, b, (((contract[0],), (contract[1],)), ((), ())), prefe...  27.9 us
    pallas_call x1, Pallas kernels, attention_back(): pl.pallas_call(kernel, out_shape=[jax.ShapeDtypeStruct((tokens, QKV_WIDTH...  20.5 us
    ppermute x14, starting transfers between devices, to_right(): return lax.ppermute(v, 'wide', self.right)  18.5 us
  transfers between devices with their start and end apart: 74, of which 30 were waited for; matrix products, arithmetic and copies ran while one was open for 15% of the time, Pallas kernels for 8%

profile of v1, /device:TPU:0, one launch (start us, length us, event | category | flops | bytes accessed | tf_op | source)
XLA Modules:
  0.0 611.2 jit_solution(17163037734989916087)
XLA Ops:
  13.9 5.2 collective-permute-done.refs_1_
  23.2 19.7 %collective-permute-done.2.refs_3_ = bf16[32,5632]{1,0:T(8,128)(2,1)S(1)} collective-permute-done((bf16[32,5632]{1,0:T(8,128)(2,1)S(1)}, bf16[32,5632]{1,0:T(8,128)(2,1)S(1)}, u32[]{:S(2)}, u32[]{:S(2)}) %collective-permute-start.2) | collective-permute-done | bytes 360480 | tf_op jit(solution)/shard_map/ppermute | solution.py:83
  52.2 5.3 collective-permute-done.4.refs_5_
  61.7 6.7 %collective-permute-done.6.refs_7_ = bf16[32,5632]{1,0:T(8,128)(2,1)S(1)} collective-permute-done((bf16[32,5632]{1,0:T(8,128)(2,1)S(1)}, bf16[32,5632]{1,0:T(8,128)(2,1)S(1)}, u32[]{:S(2)}, u32[]{:S(2)}) %collective-permute-start.6) | collective-permute-done | bytes 360480 | tf_op jit(solution)/shard_map/ppermute | solution.py:83
  70.3 27.3 %collective-permute-done.9.refs_10_ = bf16[64,5632]{1,0:T(8,128)(2,1)} collective-permute-done((bf16[64,5632]{1,0:T(8,128)(2,1)S(1)}, bf16[64,5632]{1,0:T(8,128)(2,1)}, u32[]{:S(2)}, u32[]{:S(2)}) %collective-permute-start.9) | collective-permute-done | bytes 720928 | tf_op jit(solution)/shard_map/ppermute | solution.py:86
  104.9 10.8 %collective-permute-done.10.refs_11_ = bf16[64,5632]{1,0:T(8,128)(2,1)} collective-permute-done((bf16[64,5632]{1,0:T(8,128)(2,1)}, bf16[64,5632]{1,0:T(8,128)(2,1)}, u32[]{:S(2)}, u32[]{:S(2)}) %collective-permute-start.10) | collective-permute-done | bytes 720928 | tf_op jit(solution)/shard_map/ppermute | solution.py:86
  134.1 9.6 %assemble.1 = (bf16[1024,2560]{1,0:T(8,128)(2,1)}, bf16[1024,2048]{1,0:T(8,128)(2,1)}, bf16[2048,512]{1,0:T(8,128)(2,1)}) custom-call(s32[2,24]{1,0:T(2,128)S(1)} %pad_add_fusion.table_ref, bf16[64,5632]{1,0:T(8,128)(2,1)} %copy-done.45, bf16[32,5632]{1,0:T(8,128)(2,1)S(1)} %collective-permute-done.refs_1_, ...), custom_call_target="tpu_custom_call" | custom-call | bytes 23068672 | tf_op jit(solution)/shard_map/assemble/pallas_call | solution.py:205
  150.6 12.2 %attention.1 = bf16[256,2048]{1,0:T(8,128)(2,1)S(1)} custom-call(bf16[256,2560]{1,0:T(8,128)(2,1)S(1)} %convolution_convert_fusion.1.q_ref.kv_ref, bf16[256,2560]{1,0:T(8,128)(2,1)S(1)} %convolution_convert_fusion.1.q_ref.kv_ref, bf16[1024,512]{1,0:T(8,128)(2,1)S(1)} %convolution_convert_fusion.5.pre_ref, s32[1280,256]{1,0:T(8,128)S(1)} %add_convert_fusion.14.allowed_ref), custom_call_target="tpu_custom_call" | custom-call | flops 2684354560 | bytes 4718592 | tf_op jit(solution)/shard_map/attention/pallas_call | solution.py:434
  174.4 15.2 %collective-permute-done.33.refs_3_.refs_4_ = bf16[3,128,1024]{2,1,0:T(8,128)(2,1)S(1)} collective-permute-done((bf16[3,128,1024]{2,1,0:T(8,128)(2,1)S(1)}, bf16[3,128,1024]{2,1,0:T(8,128)(2,1)S(1)}, u32[]{:S(2)}, u32[]{:S(2)}) %collective-permute-start.33) | collective-permute-done | bytes 786464 | tf_op jit(solution)/shard_map/ppermute | solution.py:92
  189.6 16.9 %collective-permute-done.34.refs_6_.refs_1_ = bf16[3,128,1024]{2,1,0:T(8,128)(2,1)S(1)} collective-permute-done((bf16[3,128,1024]{2,1,0:T(8,128)(2,1)}, bf16[3,128,1024]{2,1,0:T(8,128)(2,1)S(1)}, u32[]{:S(2)}, u32[]{:S(2)}) %collective-permute-start.34) | collective-permute-done | bytes 786464 | tf_op jit(solution)/shard_map/ppermute | solution.py:92
  206.5 9.2 %ff_forward.2 = (f32[5,512,256]{2,1,0:T(8,128)}, f32[5,512,256]{2,1,0:T(8,128)}, bf16[5,512,256]{2,1,0:T(8,128)(2,1)}, f32[256,1024]{1,0:T(8,128)S(1)}, f32[256,1024]{1,0:T(8,128)S(1)}) custom-call(bf16[512,1024]{1,0:T(8,128)(2,1)} %pad_maximum_fusion.1.norm_ref, bf16[3,256,1024]{2,1,0:T(8,128)(2,1)} %copy-done.55, bf16[3,256,1024]{2,1,0:T(8,128)(2,1)} %copy-done.92, ...), custom_call_target="tpu_custom_call" | custom-call | flops 4026531840 | bytes 14417920 | tf_op jit(solution)/shard_map/ff_forward/pallas_call | solution.py:290
  217.7 5.7 collective-permute-done.30.refs_2_.refs_3_
  223.3 16.4 %collective-permute-done.32.refs_4_.refs_1_ = bf16[3,128,1024]{2,1,0:T(8,128)(2,1)S(1)} collective-permute-done((bf16[3,128,1024]{2,1,0:T(8,128)(2,1)S(1)}, bf16[3,128,1024]{2,1,0:T(8,128)(2,1)S(1)}, u32[]{:S(2)}, u32[]{:S(2)}) %collective-permute-start.32) | collective-permute-done | bytes 786464 | tf_op jit(solution)/shard_map/ppermute | solution.py:92
  240.9 7.4 %ff_forward.3 = (f32[3,512,256]{2,1,0:T(8,128)}, f32[3,512,256]{2,1,0:T(8,128)}, bf16[3,512,256]{2,1,0:T(8,128)(2,1)S(1)}, f32[256,1024]{1,0:T(8,128)S(1)}, f32[256,1024]{1,0:T(8,128)S(1)}) custom-call(bf16[512,1024]{1,0:T(8,128)(2,1)} %pad_maximum_fusion.1.norm_ref, bf16[3,256,1024]{2,1,0:T(8,128)(2,1)} %copy-done.93, ...), custom_call_target="tpu_custom_call" | custom-call | flops 2415919104 | bytes 8650752 | tf_op jit(solution)/shard_map/ff_forward/pallas_call | solution.py:290
  258.2 13.4 %ff_backward.2 = (bf16[3,128,1024]{2,1,0:T(8,128)(2,1)S(1)}, bf16[3,128,1024]{2,1,0:T(8,128)(2,1)S(1)}, bf16[3,128,1024]{2,1,0:T(8,128)(2,1)S(1)}, bf16[3,128,10...) custom-call(bf16[512,1024]{1,0:T(8,128)(2,1)} %pad_maximum_fusion.1.norm_ref, ...), custom_call_target="tpu_custom_call" | custom-call | flops 4831838208 | bytes 13369344 | tf_op jit(solution)/shard_map/ff_backward/pallas_call | solution.py:390
  272.5 20.9 %ff_backward.3 = (bf16[3,128,1024]{2,1,0:T(8,128)(2,1)S(1)}, bf16[3,128,1024]{2,1,0:T(8,128)(2,1)S(1)}, bf16[3,256,1024]{2,1,0:T(8,128)(2,1)}, bf16[3,128,1024]{...) custom-call(bf16[512,1024]{1,0:T(8,128)(2,1)} %pad_maximum_fusion.1., ...), custom_call_target="tpu_custom_call" | custom-call | flops 8053063680 | bytes 22282240 | tf_op jit(solution)/shard_map/ff_backward/pallas_call | solution.py:390
  309.8 20.5 %attention_back.1 = (bf16[256,2560]{1,0:T(8,128)(2,1)S(1)}, bf16[1024,512]{1,0:T(8,128)(2,1)S(1)}) custom-call(bf16[256,2560]{1,0:T(8,128)(2,1)S(1)} %copy-done.30, bf16[256,2560]{1,0:T(8,128)(2,1)S(1)} %copy-done.30, bf16[1024,512]{1,0:T(8,128)(2,1)S(1)} %copy-done.32, s32[1280,256]{1,0:T(8,128)} %copy-done, ...), custom_call_target="tpu_custom_call" | custom-call | flops 6710886400 | bytes 8126464 | tf_op jit(solution)/shard_map/attention_back/pallas_call | solution.py:493
  334.7 4.5 fusion.14
  363.9 4.8 convolution_convert_fusion.2
  372.3 4.4 reshape.230
  390.9 6.2 %collective-permute-done.41 = f32[39,1024]{1,0:T(8,128)S(1)} collective-permute-done((f32[39,1024]{1,0:T(8,128)S(1)}, f32[39,1024]{1,0:T(8,128)S(1)}, u32[]{:S(2)}, u32[]{:S(2)}) %collective-permute-start.41) | collective-permute-done | bytes 159776 | tf_op jit(solution)/shard_map/ppermute | solution.py:156
  401.2 19.5 %collective-permute-done.42 = f32[39,1024]{1,0:T(8,128)S(1)} collective-permute-done((f32[39,1024]{1,0:T(8,128)S(1)}, f32[39,1024]{1,0:T(8,128)S(1)}, u32[]{:S(2)}, u32[]{:S(2)}) %collective-permute-start.42) | collective-permute-done | bytes 159776 | tf_op jit(solution)/shard_map/ppermute | solution.py:92
  432.7 16.1 %collective-permute-done.54 = bf16[32,5632]{1,0:T(8,128)(2,1)S(1)} collective-permute-done((bf16[32,5632]{1,0:T(8,128)(2,1)S(1)}, bf16[32,5632]{1,0:T(8,128)(2,1)S(1)}, u32[]{:S(2)}, u32[]{:S(2)}) %collective-permute-start.54) | collective-permute-done | bytes 360480 | tf_op jit(solution)/shard_map/ppermute | solution.py:92
  458.9 41.1 %collective-permute-done.48 = bf16[64,5632]{1,0:T(8,128)(2,1)S(1)} collective-permute-done((bf16[64,5632]{1,0:T(8,128)(2,1)S(1)}, bf16[64,5632]{1,0:T(8,128)(2,1)S(1)}, u32[]{:S(2)}, u32[]{:S(2)}) %collective-permute-start.48) | collective-permute-done | bytes 720928 | tf_op jit(solution)/shard_map/ppermute | solution.py:83
  503.0 8.4 %collective-permute-done.56 = bf16[32,5632]{1,0:T(8,128)(2,1)S(1)} collective-permute-done((bf16[32,5632]{1,0:T(8,128)(2,1)S(1)}, bf16[32,5632]{1,0:T(8,128)(2,1)S(1)}, u32[]{:S(2)}, u32[]{:S(2)}) %collective-permute-start.56) | collective-permute-done | bytes 360480 | tf_op jit(solution)/shard_map/ppermute | solution.py:86
  511.9 16.6 %collective-permute-done.49 = bf16[64,5632]{1,0:T(8,128)(2,1)S(1)} collective-permute-done((bf16[64,5632]{1,0:T(8,128)(2,1)S(1)}, bf16[64,5632]{1,0:T(8,128)(2,1)S(1)}, u32[]{:S(2)}, u32[]{:S(2)}) %collective-permute-start.49) | collective-permute-done | bytes 720928 | tf_op jit(solution)/shard_map/ppermute | solution.py:83
  530.8 7.9 %collective-permute-done.57 = bf16[32,5632]{1,0:T(8,128)(2,1)S(1)} collective-permute-done((bf16[32,5632]{1,0:T(8,128)(2,1)S(1)}, bf16[32,5632]{1,0:T(8,128)(2,1)S(1)}, u32[]{:S(2)}, u32[]{:S(2)}) %collective-permute-start.57) | collective-permute-done | bytes 360480 | tf_op jit(solution)/shard_map/ppermute | solution.py:86
  539.6 6.5 %collective-permute-done.50 = bf16[64,5632]{1,0:T(8,128)(2,1)S(1)} collective-permute-done((bf16[64,5632]{1,0:T(8,128)(2,1)S(1)}, bf16[64,5632]{1,0:T(8,128)(2,1)S(1)}, u32[]{:S(2)}, u32[]{:S(2)}) %collective-permute-start.50) | collective-permute-done | bytes 720928 | tf_op jit(solution)/shard_map/ppermute | solution.py:83
  556.6 17.3 %collective-permute-done.63 = bf16[3,256,1024]{2,1,0:T(8,128)(2,1)S(1)} collective-permute-done((bf16[3,256,1024]{2,1,0:T(8,128)(2,1)S(1)}, bf16[3,256,1024]{2,1,0:T(8,128)(2,1)S(1)}, u32[]{:S(2)}, u32[]{:S(2)}) %collective-permute-start.63) | collective-permute-done | bytes 1572896 | tf_op jit(solution)/shard_map/ppermute | solution.py:83
  578.5 14.3 %collective-permute-done.72 = bf16[3,128,1024]{2,1,0:T(8,128)(2,1)S(1)} collective-permute-done((bf16[3,128,1024]{2,1,0:T(8,128)(2,1)S(1)}, bf16[3,128,1024]{2,1,0:T(8,128)(2,1)S(1)}, u32[]{:S(2)}, u32[]{:S(2)}) %collective-permute-start.72) | collective-permute-done | bytes 786464 | tf_op jit(solution)/shard_map/ppermute | solution.py:92
  598.3 7.1 %collective-permute-done.73 = bf16[3,128,1024]{2,1,0:T(8,128)(2,1)S(1)} collective-permute-done((bf16[3,128,1024]{2,1,0:T(8,128)(2,1)S(1)}, bf16[3,128,1024]{2,1,0:T(8,128)(2,1)S(1)}, u32[]{:S(2)}, u32[]{:S(2)}) %collective-permute-start.73) | collective-permute-done | bytes 786464 | tf_op jit(solution)/shard_map/ppermute | solution.py:92
  605.3 4.5 multiply_add_fusion
  (415 shorter events, 189.7 us)
Async XLA Ops:
  12.3 36.6 %collective-permute-start.27 = (bf16[3,128,1024]{2,1,0:T(8,128)(2,1)S(1)}, bf16[3,128,1024]{2,1,0:T(8,128)(2,1)S(1)}, u32[]{:S(2)}, u32[]{:S(2)}) collective-permute-start(bf16[3,128,1024]{2,1,0:T(8,128)(2,1)S(1)} %dynamic-slice_bitcast_fusion.1), channel_id=1, source_target_pairs={{0,4},{1,5},{4,8},{5,9},{8,12},{9,13},{12,14},{13,15},{14,10},{15,... | collective-permute-start | bytes 2359304 | tf_op jit(solution)/shard_map/ppermute | solution.py:83
  21.2 26.0 %collective-permute-start.8 = (bf16[64,5632]{1,0:T(8,128)(2,1)}, bf16[64,5632]{1,0:T(8,128)(2,1)S(1)}, u32[]{:S(2)}, u32[]{:S(2)}) collective-permute-start(bf16[64,5632]{1,0:T(8,128)(2,1)} %copy-done.45), channel_id=1, source_target_pairs={{4,0},{5,1},{8,4},{9,5},{12,8},{13,9},{14,12},{15,13},{10,14},{11,... | collective-permute-start | bytes 2162696 | tf_op jit(solution)/shard_map/ppermute | solution.py:86
  21.2 27.7 %collective-permute-start.11 = (bf16[64,5632]{1,0:T(8,128)(2,1)}, bf16[64,5632]{1,0:T(8,128)(2,1)S(1)}, u32[]{:S(2)}, u32[]{:S(2)}) collective-permute-start(bf16[64,5632]{1,0:T(8,128)(2,1)} %copy-done.45), channel_id=1, source_target_pairs={{0,1},{1,0},{2,3},{3,2},{4,5},{5,4},{6,7},{7,6},{8,9},{9,8},{10,11... | collective-permute-start | bytes 2162696 | tf_op jit(solution)/shard_map/ppermute | solution.py:89
  45.1 58.9 %collective-permute-start.24 = (bf16[3,256,1024]{2,1,0:T(8,128)(2,1)S(1)}, bf16[3,256,1024]{2,1,0:T(8,128)(2,1)S(1)}, u32[]{:S(2)}, u32[]{:S(2)}) collective-permute-start(bf16[3,256,1024]{2,1,0:T(8,128)(2,1)S(1)} %convert_bitcast_fusion.refs_0_.refs_6_), channel_id=1, source_target_pairs={{4,0},{5,1},{8,4},{9,5},{12,8},{13,9},{14,12},{15,13},{10,14},{11,... | collective-permute-start | bytes 4718600 | tf_op jit(solution)/shard_map/ppermute | solution.py:86
  49.8 47.8 %collective-permute-start.9 = (bf16[64,5632]{1,0:T(8,128)(2,1)S(1)}, bf16[64,5632]{1,0:T(8,128)(2,1)}, u32[]{:S(2)}, u32[]{:S(2)}) collective-permute-start(bf16[64,5632]{1,0:T(8,128)(2,1)S(1)} %collective-permute-done.8.refs_9_), channel_id=1, source_target_pairs={{4,0},{5,1},{8,4},{9,5},{12,8},{13,9},{14,12},{15,13},{10,14},{11,... | collective-permute-start | bytes 2162696 | tf_op jit(solution)/shard_map/ppermute | solution.py:86
  61.5 38.0 %collective-permute-start.16 = (bf16[32,5632]{1,0:T(8,128)(2,1)S(1)}, bf16[32,5632]{1,0:T(8,128)(2,1)S(1)}, u32[]{:S(2)}, u32[]{:S(2)}) collective-permute-start(bf16[32,5632]{1,0:T(8,128)(2,1)S(1)} %collective-permute-done.4.refs_5_), channel_id=1, source_target_pairs={{0,1},{1,0},{2,3},{3,2},{4,5},{5,4},{6,7},{7,6},{8,9},{9,8},{10,11... | collective-permute-start | bytes 1081352 | tf_op jit(solution)/shard_map/ppermute | solution.py:89
  68.4 35.2 %collective-permute-start.20 = (bf16[64,5632]{1,0:T(8,128)(2,1)S(1)}, bf16[64,5632]{1,0:T(8,128)(2,1)S(1)}, u32[]{:S(2)}, u32[]{:S(2)}) collective-permute-start(bf16[64,5632]{1,0:T(8,128)(2,1)S(1)} %collective-permute-done.8.refs_9_), channel_id=1, source_target_pairs={{0,1},{1,0},{2,3},{3,2},{4,5},{5,4},{6,7},{7,6},{8,9},{9,8},{10,11... | collective-permute-start | bytes 2162696 | tf_op jit(solution)/shard_map/ppermute | solution.py:89
  68.6 34.9 %collective-permute-start.28 = (bf16[3,128,1024]{2,1,0:T(8,128)(2,1)S(1)}, bf16[3,128,1024]{2,1,0:T(8,128)(2,1)}, u32[]{:S(2)}, u32[]{:S(2)}) collective-permute-start(bf16[3,128,1024]{2,1,0:T(8,128)(2,1)S(1)} %collective-permute-done.27.refs_2_.refs_3_), channel_id=1, source_target_pairs={{0,4},{1,5},{4,8},{5,9},{8,12},{9,13},{12,14},{13,15},{14,10},{15,... | collective-permute-start | bytes 2359304 | tf_op jit(solution)/shard_map/ppermute | solution.py:83
  103.6 27.6 %collective-permute-start.21 = (bf16[64,5632]{1,0:T(8,128)(2,1)}, bf16[64,5632]{1,0:T(8,128)(2,1)}, u32[]{:S(2)}, u32[]{:S(2)}) collective-permute-start(bf16[64,5632]{1,0:T(8,128)(2,1)} %collective-permute-done.9.refs_10_), channel_id=1, source_target_pairs={{0,1},{1,0},{2,3},{3,2},{4,5},{5,4},{6,7},{7,6},{8,9},{9,8},{10,11... | collective-permute-start | bytes 2162696 | tf_op jit(solution)/shard_map/ppermute | solution.py:89
  104.4 26.0 %collective-permute-start.29 = (bf16[3,128,1024]{2,1,0:T(8,128)(2,1)}, bf16[3,128,1024]{2,1,0:T(8,128)(2,1)}, u32[]{:S(2)}, u32[]{:S(2)}) collective-permute-start(bf16[3,128,1024]{2,1,0:T(8,128)(2,1)} %collective-permute-done.28.refs_5_.refs_0_), channel_id=1, source_target_pairs={{0,4},{1,5},{4,8},{5,9},{8,12},{9,13},{12,14},{13,15},{14,10},{15,... | collective-permute-start | bytes 2359304 | tf_op jit(solution)/shard_map/ppermute | solution.py:83
  128.8 38.0 %collective-permute-start.25 = (bf16[3,256,1024]{2,1,0:T(8,128)(2,1)}, bf16[3,256,1024]{2,1,0:T(8,128)(2,1)}, u32[]{:S(2)}, u32[]{:S(2)}) collective-permute-start(bf16[3,256,1024]{2,1,0:T(8,128)(2,1)} %copy-done.92), channel_id=1, source_target_pairs={{4,0},{5,1},{8,4},{9,5},{12,8},{13,9},{14,12},{15,13},{10,14},{11,... | collective-permute-start | bytes 4718600 | tf_op jit(solution)/shard_map/ppermute | solution.py:86
  130.4 40.9 %collective-permute-start.31 = (bf16[3,128,1024]{2,1,0:T(8,128)(2,1)}, bf16[3,128,1024]{2,1,0:T(8,128)(2,1)S(1)}, u32[]{:S(2)}, u32[]{:S(2)}) collective-permute-start(bf16[3,128,1024]{2,1,0:T(8,128)(2,1)} %collective-permute-done.29.refs_1_.refs_2_), channel_id=1, source_target_pairs={{0,4},{1,5},{4,8},{5,9},{8,12},{9,13},{12,14},{13,15},{14,10},{15,... | collective-permute-start | bytes 2359304 | tf_op jit(solution)/shard_map/ppermute | solution.py:83
  166.8 72.9 %collective-permute-start.26 = (bf16[3,256,1024]{2,1,0:T(8,128)(2,1)}, bf16[3,256,1024]{2,1,0:T(8,128)(2,1)S(1)}, u32[]{:S(2)}, u32[]{:S(2)}) collective-permute-start(bf16[3,256,1024]{2,1,0:T(8,128)(2,1)} %collective-permute-done.25.refs_4_.refs_2_), channel_id=1, source_target_pairs={{4,0},{5,1},{8,4},{9,5},{12,8},{13,9},{14,12},{15,13},{10,14},{11,... | collective-permute-start | bytes 4718600 | tf_op jit(solution)/shard_map/ppermute | solution.py:86
  170.8 35.7 %collective-permute-start.34 = (bf16[3,128,1024]{2,1,0:T(8,128)(2,1)}, bf16[3,128,1024]{2,1,0:T(8,128)(2,1)S(1)}, u32[]{:S(2)}, u32[]{:S(2)}) collective-permute-start(bf16[3,128,1024]{2,1,0:T(8,128)(2,1)} %collective-permute-done.28.refs_5_.refs_0_), channel_id=1, source_target_pairs={{0,16},{16,0},{1,17},{17,1},{2,18},{18,2},{3,19},{19,3},{4,20},{20... | collective-permute-start | bytes 2359304 | tf_op jit(solution)/shard_map/ppermute | solution.py:92
  171.3 52.0 %collective-permute-start.30 = (bf16[3,128,1024]{2,1,0:T(8,128)(2,1)}, bf16[3,128,1024]{2,1,0:T(8,128)(2,1)S(1)}, u32[]{:S(2)}, u32[]{:S(2)}) collective-permute-start(bf16[3,128,1024]{2,1,0:T(8,128)(2,1)} %collective-permute-done.29.refs_1_.refs_2_), channel_id=1, source_target_pairs={{0,16},{16,0},{1,17},{17,1},{2,18},{18,2},{3,19},{19,3},{4,20},{20... | collective-permute-start | bytes 2359304 | tf_op jit(solution)/shard_map/ppermute | solution.py:92
  172.8 66.9 %collective-permute-start.32 = (bf16[3,128,1024]{2,1,0:T(8,128)(2,1)S(1)}, bf16[3,128,1024]{2,1,0:T(8,128)(2,1)S(1)}, u32[]{:S(2)}, u32[]{:S(2)}) collective-permute-start(bf16[3,128,1024]{2,1,0:T(8,128)(2,1)S(1)} %collective-permute-done.31.refs_3_.refs_0_), channel_id=1, source_target_pairs={{0,16},{16,0},{1,17},{17,1},{2,18},{18,2},{3,19},{19,3},{4,20},{20... | collective-permute-start | bytes 2359304 | tf_op jit(solution)/shard_map/ppermute | solution.py:92
  301.1 55.8 %collective-permute-start.67 = (bf16[3,128,1024]{2,1,0:T(8,128)(2,1)}, bf16[3,128,1024]{2,1,0:T(8,128)(2,1)}, u32[]{:S(2)}, u32[]{:S(2)}) collective-permute-start(bf16[3,128,1024]{2,1,0:T(8,128)(2,1)} %copy-done.24), channel_id=1, source_target_pairs={{0,16},{16,0},{1,17},{17,1},{2,18},{18,2},{3,19},{19,3},{4,20},{20... | collective-permute-start | bytes 2359304 | tf_op jit(solution)/shard_map/ppermute | solution.py:92
  302.7 83.3 %collective-permute-start.61 = (bf16[3,256,1024]{2,1,0:T(8,128)(2,1)}, bf16[3,256,1024]{2,1,0:T(8,128)(2,1)}, u32[]{:S(2)}, u32[]{:S(2)}) collective-permute-start(bf16[3,256,1024]{2,1,0:T(8,128)(2,1)} %get-tuple-element.72), channel_id=1, source_target_pairs={{0,4},{1,5},{4,8},{5,9},{8,12},{9,13},{12,14},{13,15},{14,10},{15,... | collective-permute-start | bytes 4718600 | tf_op jit(solution)/shard_map/ppermute | solution.py:83
  352.8 26.3 %collective-permute-start.46 = (bf16[256,2048]{1,0:T(8,128)(2,1)}, bf16[256,2048]{1,0:T(8,128)(2,1)}, u32[]{:S(2)}, u32[]{:S(2)}) collective-permute-start(bf16[256,2048]{1,0:T(8,128)(2,1)} %copy-done.15), channel_id=1, source_target_pairs={{0,1},{1,0},{2,3},{3,2},{4,5},{5,4},{6,7},{7,6},{8,9},{9,8},{10,11... | collective-permute-start | bytes 3145736 | tf_op jit(solution)/shard_map/ppermute | solution.py:89
  353.3 43.8 %collective-permute-start.66 = (bf16[3,128,1024]{2,1,0:T(8,128)(2,1)}, bf16[3,128,1024]{2,1,0:T(8,128)(2,1)}, u32[]{:S(2)}, u32[]{:S(2)}) collective-permute-start(bf16[3,128,1024]{2,1,0:T(8,128)(2,1)} %copy-done.23), channel_id=1, source_target_pairs={{0,16},{16,0},{1,17},{17,1},{2,18},{18,2},{3,19},{19,3},{4,20},{20... | collective-permute-start | bytes 2359304 | tf_op jit(solution)/shard_map/ppermute | solution.py:92
  359.3 39.5 %collective-permute-start.68 = (bf16[3,128,1024]{2,1,0:T(8,128)(2,1)}, bf16[3,128,1024]{2,1,0:T(8,128)(2,1)}, u32[]{:S(2)}, u32[]{:S(2)}) collective-permute-start(bf16[3,128,1024]{2,1,0:T(8,128)(2,1)} %add_convert_fusion.7), channel_id=1, source_target_pairs={{4,0},{5,1},{8,4},{9,5},{12,8},{13,9},{14,12},{15,13},{10,14},{11,... | collective-permute-start | bytes 2359304 | tf_op jit(solution)/shard_map/ppermute | solution.py:86
  379.2 47.1 %collective-permute-start.44 = (bf16[256,2560]{1,0:T(8,128)(2,1)S(1)}, bf16[256,2560]{1,0:T(8,128)(2,1)S(1)}, u32[]{:S(2)}, u32[]{:S(2)}) collective-permute-start(bf16[256,2560]{1,0:T(8,128)(2,1)S(1)} %copy-done.14), channel_id=1, source_target_pairs={{0,1},{1,0},{2,3},{3,2},{4,5},{5,4},{6,7},{7,6},{8,9},{9,8},{10,11... | collective-permute-start | bytes 3932168 | tf_op jit(solution)/shard_map/ppermute | solution.py:89
  386.0 38.4 %collective-permute-start.47 = (bf16[512,1024]{1,0:T(8,128)(2,1)S(1)}, bf16[512,1024]{1,0:T(8,128)(2,1)S(1)}, u32[]{:S(2)}, u32[]{:S(2)}) collective-permute-start(bf16[512,1024]{1,0:T(8,128)(2,1)S(1)} %dynamic-slice_bitcast_fusion), channel_id=1, source_target_pairs={{0,1},{1,0},{2,3},{3,2},{4,5},{5,4},{6,7},{7,6},{8,9},{9,8},{10,11... | collective-permute-start | bytes 3145736 | tf_op jit(solution)/shard_map/ppermute | solution.py:89
  397.1 29.2 %collective-permute-start.43 = (bf16[256,512]{0,1:T(8,128)(2,1)S(1)}, bf16[256,512]{0,1:T(8,128)(2,1)S(1)}, u32[]{:S(2)}, u32[]{:S(2)}) collective-permute-start(bf16[256,512]{0,1:T(8,128)(2,1)S(1)} %copy-done.70), channel_id=1, source_target_pairs={{0,1},{1,0},{2,3},{3,2},{4,5},{5,4},{6,7},{7,6},{8,9},{9,8},{10,11... | collective-permute-start | bytes 786440 | tf_op jit(solution)/shard_map/ppermute | solution.py:89
  397.1 53.6 %collective-permute-start.65 = (bf16[3,128,1024]{2,1,0:T(8,128)(2,1)S(1)}, bf16[3,128,1024]{2,1,0:T(8,128)(2,1)S(1)}, u32[]{:S(2)}, u32[]{:S(2)}) collective-permute-start(bf16[3,128,1024]{2,1,0:T(8,128)(2,1)S(1)} %copy-done.22), channel_id=1, source_target_pairs={{0,16},{16,0},{1,17},{17,1},{2,18},{18,2},{3,19},{19,3},{4,20},{20... | collective-permute-start | bytes 2359304 | tf_op jit(solution)/shard_map/ppermute | solution.py:92
  420.7 131.6 %collective-permute-start.64 = (bf16[3,128,1024]{2,1,0:T(8,128)(2,1)S(1)}, bf16[3,128,1024]{2,1,0:T(8,128)(2,1)S(1)}, u32[]{:S(2)}, u32[]{:S(2)}) collective-permute-start(bf16[3,128,1024]{2,1,0:T(8,128)(2,1)S(1)} %copy-done.20), channel_id=1, source_target_pairs={{0,16},{16,0},{1,17},{17,1},{2,18},{18,2},{3,19},{19,3},{4,20},{20... | collective-permute-start | bytes 2359304 | tf_op jit(solution)/shard_map/ppermute | solution.py:92
  424.3 27.1 %collective-permute-start.69 = (bf16[3,128,1024]{2,1,0:T(8,128)(2,1)S(1)}, bf16[3,128,1024]{2,1,0:T(8,128)(2,1)S(1)}, u32[]{:S(2)}, u32[]{:S(2)}) collective-permute-start(bf16[3,128,1024]{2,1,0:T(8,128)(2,1)S(1)} %add_convert_fusion.6), channel_id=1, source_target_pairs={{4,0},{5,1},{8,4},{9,5},{12,8},{13,9},{14,12},{15,13},{10,14},{11,... | collective-permute-start | bytes 2359304 | tf_op jit(solution)/shard_map/ppermute | solution.py:86
  450.7 98.3 %collective-permute-start.62 = (bf16[3,256,1024]{2,1,0:T(8,128)(2,1)S(1)}, bf16[3,256,1024]{2,1,0:T(8,128)(2,1)S(1)}, u32[]{:S(2)}, u32[]{:S(2)}) collective-permute-start(bf16[3,256,1024]{2,1,0:T(8,128)(2,1)S(1)} %add_convert_fusion.2), channel_id=1, source_target_pairs={{0,4},{1,5},{4,8},{5,9},{8,12},{9,13},{12,14},{13,15},{14,10},{15,... | collective-permute-start | bytes 4718600 | tf_op jit(solution)/shard_map/ppermute | solution.py:83
  451.4 49.4 %collective-permute-start.52 = (bf16[32,5632]{1,0:T(8,128)(2,1)S(1)}, bf16[32,5632]{1,0:T(8,128)(2,1)S(1)}, u32[]{:S(2)}, u32[]{:S(2)}) collective-permute-start(bf16[32,5632]{1,0:T(8,128)(2,1)S(1)} %get-tuple-element.108), channel_id=1, source_target_pairs={{0,16},{16,0},{1,17},{17,1},{2,18},{18,2},{3,19},{19,3},{4,20},{20... | collective-permute-start | bytes 1081352 | tf_op jit(solution)/shard_map/ppermute | solution.py:92
  456.6 72.2 %collective-permute-start.51 = (bf16[32,5632]{1,0:T(8,128)(2,1)S(1)}, bf16[32,5632]{1,0:T(8,128)(2,1)S(1)}, u32[]{:S(2)}, u32[]{:S(2)}) collective-permute-start(bf16[32,5632]{1,0:T(8,128)(2,1)S(1)} %get-tuple-element.105), channel_id=1, source_target_pairs={{0,16},{16,0},{1,17},{17,1},{2,18},{18,2},{3,19},{19,3},{4,20},{20... | collective-permute-start | bytes 1081352 | tf_op jit(solution)/shard_map/ppermute | solution.py:92
  458.1 41.9 %collective-permute-start.48 = (bf16[64,5632]{1,0:T(8,128)(2,1)S(1)}, bf16[64,5632]{1,0:T(8,128)(2,1)S(1)}, u32[]{:S(2)}, u32[]{:S(2)}) collective-permute-start(bf16[64,5632]{1,0:T(8,128)(2,1)S(1)} %constant_dynamic-slice_fusion.2), channel_id=1, source_target_pairs={{0,4},{1,5},{4,8},{5,9},{8,12},{9,13},{12,14},{13,15},{14,10},{15,... | collective-permute-start | bytes 2162696 | tf_op jit(solution)/shard_map/ppermute | solution.py:83
  500.8 51.5 %collective-permute-start.70 = (bf16[3,128,1024]{2,1,0:T(8,128)(2,1)S(1)}, bf16[3,128,1024]{2,1,0:T(8,128)(2,1)S(1)}, u32[]{:S(2)}, u32[]{:S(2)}) collective-permute-start(bf16[3,128,1024]{2,1,0:T(8,128)(2,1)S(1)} %add_convert_fusion.5), channel_id=1, source_target_pairs={{4,0},{5,1},{8,4},{9,5},{12,8},{13,9},{14,12},{15,13},{10,14},{11,... | collective-permute-start | bytes 2359304 | tf_op jit(solution)/shard_map/ppermute | solution.py:86
  (137 other events, 2188.6 us)

commit v2 on v1

v2 whole, which is shorter than its diff:
```python
import functools
import math

import jax
import jax.numpy as jnp
import numpy as np
from jax import lax
from jax.experimental import pallas as pl
from jax.experimental.pallas import tpu as pltpu
from jax.sharding import PartitionSpec as P

HEADS = 8
HEAD_DIM = 256
QUERY_WIDTH = HEADS * HEAD_DIM
QKV_WIDTH = QUERY_WIDTH + 2 * HEAD_DIM
SCORE_SCALE = HEAD_DIM ** (-0.5)

NORM_EPSILON = 1e-06
MOMENTUM = 0.9
AVERAGE_DECAY = 0.8
NEGATIVE = -1e30

bf16 = jnp.bfloat16
f32 = jnp.float32
HIGHEST = lax.Precision.HIGHEST
VMEM_LIMIT = 48 * 2**20
BRIEF = pl.CostEstimate(flops=1, transcendentals=0, bytes_accessed=1)


def rms_norm(stream, gain_row):
    return (
        stream
        * lax.rsqrt(jnp.mean(stream * stream, axis=-1, keepdims=True) + NORM_EPSILON)
        * (1.0 + gain_row)
    )


def norm_back(stream, gain_row, cotangent):
    _, pull = jax.vjp(rms_norm, stream, gain_row)
    return pull(cotangent)


def gated_unit(gate_value, linear_value):
    return jax.nn.gelu(gate_value, approximate=True) * linear_value


def visible(prefix_ids, action_ids, block_flags):
    length = block_flags.shape[0]
    place = jnp.arange(length)
    upto = place[None, :] <= place[:, None]
    levels = jnp.sum(jnp.where(upto, block_flags[None, :], 0), axis=1)
    from_prefix = prefix_ids[:, None] == action_ids[None, :]
    from_action = (action_ids[:, None] == action_ids[None, :]) & (
        levels[:, None] <= levels[None, :]
    )
    return jnp.concatenate([from_prefix, from_action], axis=0).astype(jnp.int32)


def advance(weight, moment, average, gradient, step_rate):
    moment_next = MOMENTUM * moment + gradient
    weight_next = weight - step_rate * (gradient + MOMENTUM * moment_next)
    average_next = AVERAGE_DECAY * average + (1.0 - AVERAGE_DECAY) * weight_next
    return (weight_next, moment_next, average_next)


def mm(a, b, contract, out=f32):
    return lax.dot_general(
        a, b, (((contract[0],), (contract[1],)), ((), ())), preferred_element_type=f32
    ).astype(out)


class Order:
    def __init__(self):
        self.token = jnp.zeros((), jnp.int32)

    def __call__(self, *values):
        *values, self.token = lax.optimization_barrier((*values, self.token))
        return values[0] if len(values) == 1 else values


class Ring:
    def __init__(self, wide):
        chips = wide // 2
        self.wide, self.chips = wide, chips
        self.cycle = list(range(0, chips, 2)) + list(range(1, chips, 2))[::-1]
        ahead = [(self.cycle[i], self.cycle[(i + 1) % chips]) for i in range(chips)]
        self.right = [(2 * s + c, 2 * t + c) for s, t in ahead for c in (0, 1)]
        self.left = [(t, s) for s, t in self.right]
        self.core = [(w, w ^ 1) for w in range(wide)]
        self.n_right = chips // 2
        self.n_left = chips - 1 - self.n_right

    def to_right(self, v):
        return lax.ppermute(v, "wide", self.right)

    def to_left(self, v):
        return lax.ppermute(v, "wide", self.left)

    def to_core(self, v):
        return lax.ppermute(v, "wide", self.core)

    def to_peer(self, v):
        return lax.ppermute(v, "batch", [(0, 1), (1, 0)])

    def owners(self, w):
        here = self.cycle.index(w // 2)
        rights = [self.cycle[(here - d) % self.chips] for d in range(1, self.n_right + 1)]
        lefts = [self.cycle[(here + d) % self.chips] for d in range(1, self.n_left + 1)]
        return [w // 2] + rights + lefts

    def bits(self):
        k, steps = 1, [self.to_peer]
        while k < self.wide:
            pairs = [(w, w ^ k) for w in range(self.wide)]
            steps.append(functools.partial(lax.ppermute, axis_name="wide", perm=pairs))
            k *= 2
        return steps


def add(*terms):
    return sum(t.astype(f32) for t in terms).astype(bf16)


class Gathering:
    def __init__(self, ring, order, axis, split_left):
        self.ring, self.order, self.axis, self.split_left = ring, order, axis, split_left
        self.blocks = {}
        self.flying = {}
        self.count = {"right": ring.n_right, "left": ring.n_left}
        self.d = {"right": 0, "left": 0}

    def halved(self, side, shard):
        half = shard.shape[self.axis] // 2
        return half % 16 == 0 and (side == "right" or self.split_left)

    def start(self, side, shard):
        cut = self.halved(side, shard)
        if cut:
            half = shard.shape[self.axis] // 2
            shard = lax.dynamic_slice_in_dim(shard, lax.axis_index("batch") * half, half, self.axis)
        self.flying[side] = (cut, self.send(side, shard))

    def send(self, side, v):
        return self.ring.to_right(v) if side == "right" else self.ring.to_left(v)

    def step(self, *sides):
        sides = [x for x in sides if self.d[x] < self.count[x]]
        for side in sides:
            cut, v = self.flying[side]
            v = self.order(v)
            d = self.d[side]
            self.blocks[side, d] = (v, self.ring.to_peer(v)) if cut else (v,)
            self.d[side] = d + 1
            if d + 1 < self.count[side]:
                self.flying[side] = (cut, self.send(side, v))

    def settle(self, *keys):
        for key in keys:
            if key in self.blocks:
                self.blocks[key] = tuple(self.order(p) for p in self.blocks[key])


class Summing:
    def __init__(self, ring, order, axis):
        self.ring, self.order, self.axis = ring, order, axis
        self.parts, self.crossed = {}, {}
        self.came = {"right": None, "left": None}
        self.d = {"right": ring.n_right - 1, "left": ring.n_left - 1}

    def put(self, key, parts):
        self.parts[key] = parts
        if len(parts) == 2:
            self.crossed[key] = self.ring.to_peer(parts[1])

    def step(self, *sides):
        for side in sides:
            d = self.d[side]
            if d < 0:
                continue
            terms = [self.parts[side, d][0]]
            terms += [self.crossed[side, d]] if (side, d) in self.crossed else []
            terms += [self.came[side]] if self.came[side] is not None else []
            terms = self.order(*terms)
            total = self.order(add(*terms)) if isinstance(terms, (list, tuple)) else terms
            self.came[side] = self.ring.to_left(total) if side == "right" else self.ring.to_right(total)
            self.d[side] = d - 1

    def ready(self, *keys):
        for key in keys:
            if key in self.crossed:
                self.crossed[key] = self.order(self.crossed[key])

    def land(self, side):
        self.came[side] = self.order(self.came[side])

    def left(self):
        return max(self.d.values()) + 1

    def own(self, shard):
        me = lax.axis_index("batch")
        half = shard.shape[self.axis] // 2
        self.ends = ["right"]
        if len(self.parts["left", 0]) == 1:
            shard = self.order(add(*self.order(shard, self.came["left"])))
        else:
            self.ends.append("left")
        self.split = len(self.parts["right", 0]) == 2
        self.mine = shard
        if self.split:
            self.mine = lax.dynamic_slice_in_dim(shard, me * half, half, self.axis)
            other = lax.dynamic_slice_in_dim(shard, (1 - me) * half, half, self.axis)
            self.mine, other = self.order(self.mine, other)
            self.across = self.ring.to_peer(other)

    def close(self):
        terms = [self.mine] + [self.came[e] for e in self.ends] + ([self.across] if self.split else [])
        self.total = self.order(add(*self.order(*terms)))
        self.across = self.ring.to_peer(self.total)

    def result(self):
        me = lax.axis_index("batch")
        total, across = self.order(self.total, self.across)
        if not self.split:
            return total.astype(f32) + across.astype(f32)
        return jnp.where(
            me == 0,
            jnp.concatenate([total, across], self.axis),
            jnp.concatenate([across, total], self.axis),
        ).astype(f32)


def packing(ring, counts, rows_a, width_a):
    half = rows_a // 2
    table = np.zeros((2, ring.wide, 2, sum(counts)), np.int32)
    for me in (0, 1):
        for w in range(ring.wide):
            where, first = [], []
            for owner, n in zip(ring.owners(w), counts):
                where += [owner] * n
                first += [me * half, (1 - me) * half] if n == 2 else [0]
            table[me, w] = where, first
    table = jnp.array(table)[lax.axis_index("batch"), lax.axis_index("wide")]

    def spots(part, chip, inner, size, width_p):
        at = pl.ds(pl.multiple_of(chip * rows_a + inner, size), size)
        pw = width_p // 2
        yield part.at[:, pl.ds(0, QKV_WIDTH)], 0, at
        yield part.at[:, pl.ds(QKV_WIDTH, width_a - QKV_WIDTH)], 1, at
        for j in (0, 1):
            to = pl.ds(pl.multiple_of(chip * (2 * rows_a) + j * rows_a + inner, size), size)
            yield part.at[:, pl.ds(width_a + j * pw, pw)], 2, to

    return table, spots


def repack(ring, blocks, arrays, rows_a, width_a, width_p):
    gather = arrays is None
    counts = [len(b) for b in blocks] if gather else blocks
    half = rows_a // 2
    table, spots = packing(ring, counts, rows_a, width_a)
    sizes = [size for n in counts for size in ([half] * 2 if n == 2 else [rows_a])]
    n = len(sizes)
    total = rows_a * ring.chips
    shapes = ((total, QKV_WIDTH), (total, width_a - QKV_WIDTH), (2 * total, width_p // 2))
    any_space = pl.BlockSpec(memory_space=pl.ANY)
    whole = [pl.BlockSpec(sh, lambda i, t: (0, 0)) for sh in shapes]

    def kernel(table_ref, *refs):
        sems = refs[-1]
        parts, full = (refs[:n], refs[n:-1]) if gather else (refs[3:-1], refs[:3])
        copies = []
        for i in range(n):
            for cut, which, rows in spots(parts[i], table_ref[0, i], table_ref[1, i], sizes[i], width_p):
                other = full[which].at[rows, :]
                pair = (cut, other) if gather else (other, cut)
                copies.append(pltpu.make_async_copy(*pair, sems.at[len(copies)]))
        for c in copies:
            c.start()
        for c in copies:
            c.wait()

    out_shapes = shapes if gather else [(size, width_a + width_p) for size in sizes]
    out = pl.pallas_call(
        kernel,
        out_shape=[jax.ShapeDtypeStruct(sh, bf16) for sh in out_shapes],
        grid_spec=pltpu.PrefetchScalarGridSpec(
            num_scalar_prefetch=1,
            grid=(1,),
            in_specs=[any_space] * n if gather else whole,
            out_specs=whole if gather else [any_space] * n,
            scratch_shapes=[pltpu.SemaphoreType.DMA((4 * n,))],
        ),
        compiler_params=pltpu.CompilerParams(vmem_limit_bytes=VMEM_LIMIT),
        cost_estimate=BRIEF,
        name="assemble" if gather else "disassemble",
    )(table, *([p for b in blocks for p in b] if gather else arrays))
    if gather:
        return out
    out = list(out)
    return [tuple(out.pop(0) for _ in range(k)) for k in counts]


def interleave(ring, own, other, rows):
    core = (lax.axis_index("wide") % 2).reshape(1)

    def kernel(core_ref, own_ref, other_ref, out_ref, sems):
        copies = []
        for chip in range(ring.chips):
            for j, ref in enumerate((own_ref, other_ref)):
                side = core_ref[0] if j == 0 else 1 - core_ref[0]
                to = pl.ds(pl.multiple_of((2 * chip + side) * rows, rows), rows)
                copies.append(
                    pltpu.make_async_copy(
                        ref.at[pl.ds(chip * rows, rows), :], out_ref.at[to, :], sems.at[chip, j]
                    )
                )
        for c in copies:
            c.start()
        for c in copies:
            c.wait()

    shape = (2 * own.shape[0], own.shape[1])
    return pl.pallas_call(
        kernel,
        out_shape=jax.ShapeDtypeStruct(shape, bf16),
        grid_spec=pltpu.PrefetchScalarGridSpec(
            num_scalar_prefetch=1,
            grid=(1,),
            in_specs=[pl.BlockSpec(memory_space=pl.ANY)] * 2,
            out_specs=pl.BlockSpec(shape, lambda i, t: (0, 0)),
            scratch_shapes=[pltpu.SemaphoreType.DMA((ring.chips, 2))],
        ),
        compiler_params=pltpu.CompilerParams(vmem_limit_bytes=VMEM_LIMIT),
        cost_estimate=BRIEF,
        name="interleave",
    )(core, own, other)


def norm_by_core(ring, rows, gains, size):
    core = (lax.axis_index("wide") % 2).reshape(1)
    tokens, dim = rows.shape
    step = 128

    def kernel(core_ref, rows_ref, gains_ref, mine_ref, other_ref):
        v = rows_ref[...].astype(f32)
        normed = rms_norm(v, gains_ref[0]).astype(bf16)
        for swapped in (0, 1):

            @pl.when(core_ref[0] == swapped)
            def _(swapped=swapped):
                for chip in range(ring.chips):
                    for side, ref in enumerate((mine_ref, other_ref)):
                        at = (2 * chip + (side ^ swapped)) * size
                        ref[:, chip * size : (chip + 1) * size] = normed[:, at : at + size]

    half = pl.BlockSpec((step, dim // 2), lambda i, t: (i, 0))
    return pl.pallas_call(
        kernel,
        out_shape=[jax.ShapeDtypeStruct((tokens, dim // 2), bf16)] * 2,
        grid_spec=pltpu.PrefetchScalarGridSpec(
            num_scalar_prefetch=1,
            grid=(tokens // step,),
            in_specs=[
                pl.BlockSpec((step, dim), lambda i, t: (i, 0)),
                pl.BlockSpec((1, dim), lambda i, t: (0, 0)),
            ],
            out_specs=[half, half],
        ),
        compiler_params=pltpu.CompilerParams(vmem_limit_bytes=VMEM_LIMIT),
        cost_estimate=BRIEF,
        name="norm_by_core",
    )(core, rows, gains)


def gelu_parts(v):
    c = math.sqrt(2.0 / math.pi)
    square = v * v
    t = jnp.tanh(c * v * (1.0 + 0.044715 * square))
    half = 0.5 * (1.0 + t)
    slope = half + 0.5 * v * (1.0 - t * t) * c * (1.0 + 3.0 * 0.044715 * square)
    return v * half, slope


def load_block(refs, buf, sems, k):
    at, made = 0, []
    for j, r in enumerate(refs):
        size = r.shape[1]
        made.append(pltpu.make_async_copy(r, buf.at[:, pl.ds(at, size), :], sems.at[k, j]))
        at += size
    return made


def ff_forward(norm_two, blocks, before):
    nb = len(blocks)
    flat = [a for blk in blocks for a in blk]
    tokens, dim = norm_two.shape
    units = sum(a.shape[1] for a in blocks[0])
    half = tokens // 2
    has_before = before is not None

    def kernel(norm_ref, *refs):
        refs = list(refs)
        ins = [[refs.pop(0) for _ in blk] for blk in blocks]
        if has_before:
            own_in, oth_in = refs.pop(0), refs.pop(0)
        gate_out, lin_out, hid_out, own_out, oth_out, buf, total, sems = refs
        i = pl.program_id(0)

        @pl.when(i == 0)
        def _():
            for k in range(nb):
                for c in load_block(ins[k], buf.at[k], sems, k):
                    c.start()
            if has_before:
                total[:half] = own_in[...]
                total[half:] = oth_in[...]
            else:
                total[...] = jnp.zeros_like(total)

        for k in range(nb):

            @pl.when(i == k)
            def _(k=k):
                for c in load_block(ins[k], buf.at[k], sems, k):
                    c.wait()

        w = buf.at[i]
        if units % 128 == 0:
            both = mm(norm_ref[...], w[:2].reshape(2 * units, dim), (1, 1))
            gate, linear = both[:, :units], both[:, units:]
        else:
            gate, linear = (mm(norm_ref[...], w[j], (1, 1)) for j in (0, 1))
        gate_out[0] = gate
        lin_out[0] = linear
        hidden = (gelu_parts(gate)[0] * linear).astype(bf16)
        hid_out[0] = hidden
        total[...] += mm(hidden, w[2], (1, 0))

        @pl.when(i == nb - 1)
        def _():
            own_out[...] = total[:half]
            oth_out[...] = total[half:]

    once = pl.BlockSpec((tokens, dim), lambda i: (0, 0))
    row = pl.BlockSpec((half, dim), lambda i: (0, 0))
    step = pl.BlockSpec((1, tokens, units), lambda i: (i, 0, 0))
    any_space = pl.BlockSpec(memory_space=pl.ANY)
    return pl.pallas_call(
        kernel,
        out_shape=[
            jax.ShapeDtypeStruct((nb, tokens, units), f32),
            jax.ShapeDtypeStruct((nb, tokens, units), f32),
            jax.ShapeDtypeStruct((nb, tokens, units), bf16),
            jax.ShapeDtypeStruct((half, dim), f32),
            jax.ShapeDtypeStruct((half, dim), f32),
        ],
        grid=(nb,),
        in_specs=[once] + [any_space] * len(flat) + [row, row] * has_before,
        out_specs=[step, step, step, row, row],
        scratch_shapes=[
            pltpu.VMEM((nb, 3, units, dim), bf16),
            pltpu.VMEM((tokens, dim), f32),
            pltpu.SemaphoreType.DMA((nb, 2)),
        ],
        compiler_params=pltpu.CompilerParams(vmem_limit_bytes=VMEM_LIMIT),
        cost_estimate=BRIEF,
        name="ff_forward",
    )(norm_two, *flat, *(before or ()))


def ff_backward(norm_two, branch_two, blocks, kept, picks, before):
    nb = len(blocks)
    flat = [a for blk in blocks for a in blk]
    gate_all, lin_all, hid_all = kept
    tokens, dim = norm_two.shape
    units = sum(a.shape[1] for a in blocks[0])
    half = tokens // 2
    has_before = before is not None
    first, stride = picks

    def kernel(norm_ref, branch_ref, gate_ref, lin_ref, hid_ref, *refs):
        refs = list(refs)
        ins = [[refs.pop(0) for _ in blk] for blk in blocks]
        if has_before:
            own_in, oth_in = refs.pop(0), refs.pop(0)
        outs = [[refs.pop(0) for _ in blk] for blk in blocks]
        own_out, oth_out, buf, grads, total, sems, out_sems = refs
        i = pl.program_id(0)

        def stores(k):
            at, made = 0, []
            for j, r in enumerate(outs[k]):
                size = r.shape[1]
                made.append(pltpu.make_async_copy(grads.at[k, :, pl.ds(at, size), :], r, out_sems.at[k, j]))
                at += size
            return made

        @pl.when(i == 0)
        def _():
            for k in range(nb):
                for c in load_block(ins[k], buf.at[k], sems, k):
                    c.start()
            if has_before:
                total[:half] = own_in[...]
                total[half:] = oth_in[...]
            else:
                total[...] = jnp.zeros_like(total)

        for k in range(nb):

            @pl.when(i == k)
            def _(k=k):
                for c in load_block(ins[k], buf.at[k], sems, k):
                    c.wait()

        w, g = buf.at[i], grads.at[i]
        back_hidden = mm(branch_ref[...], w[2], (1, 1))
        value, slope = gelu_parts(gate_ref[0])
        back_gate = (back_hidden * lin_ref[0] * slope).astype(bf16)
        back_linear = (back_hidden * value).astype(bf16)
        if units % 128 == 0:
            both = jnp.concatenate([back_gate, back_linear], 1)
            g[:2] = mm(both, norm_ref[...], (0, 0), bf16).reshape(2, units, dim)
            total[...] += mm(both, w[:2].reshape(2 * units, dim), (1, 0))
        else:
            for j, back in enumerate((back_gate, back_linear)):
                g[j] = mm(back, norm_ref[...], (0, 0), bf16)
                total[...] += mm(back, w[j], (1, 0))
        g[2] = mm(hid_ref[0], branch_ref[...], (0, 0), bf16)

        for k in range(nb):

            @pl.when(i == k)
            def _(k=k):
                for c in stores(k):
                    c.start()

        @pl.when(i == nb - 1)
        def _():
            own_out[...] = total[:half]
            oth_out[...] = total[half:]
            for k in range(nb):
                for c in stores(k):
                    c.wait()

    once = pl.BlockSpec((tokens, dim), lambda i: (0, 0))
    row = pl.BlockSpec((half, dim), lambda i: (0, 0))
    step = pl.BlockSpec((1, tokens, units), lambda i: (first + stride * i, 0, 0))
    any_space = pl.BlockSpec(memory_space=pl.ANY)
    made = pl.pallas_call(
        kernel,
        out_shape=[jax.ShapeDtypeStruct(a.shape, bf16) for a in flat]
        + [jax.ShapeDtypeStruct((half, dim), f32)] * 2,
        grid=(nb,),
        in_specs=[once, once, step, step, step] + [any_space] * len(flat) + [row, row] * has_before,
        out_specs=[any_space] * len(flat) + [row, row],
        scratch_shapes=[
            pltpu.VMEM((nb, 3, units, dim), bf16),
            pltpu.VMEM((nb, 3, units, dim), bf16),
            pltpu.VMEM((tokens, dim), f32),
            pltpu.SemaphoreType.DMA((nb, 2)),
            pltpu.SemaphoreType.DMA((nb, 2)),
        ],
        compiler_params=pltpu.CompilerParams(vmem_limit_bytes=VMEM_LIMIT),
        cost_estimate=BRIEF,
        name="ff_backward",
    )(norm_two, branch_two, gate_all, lin_all, hid_all, *flat, *(before or ()))
    made = list(made)
    grads = [tuple(made.pop(0) for _ in blk) for blk in blocks]
    return grads, made


def attention(action_qkv, prefix_kv, allowed):
    tokens, keys = action_qkv.shape[0], allowed.shape[0]
    n_pre = prefix_kv.shape[0]

    def kernel(q_ref, kv_ref, pre_ref, allowed_ref, out_ref, k_all, v_turned):
        @pl.when(pl.program_id(0) == 0)
        def _():
            k_all[:n_pre] = pre_ref[:, :HEAD_DIM]
            k_all[n_pre:] = kv_ref[:, :HEAD_DIM]
            v_turned[:, :n_pre] = pre_ref[:, HEAD_DIM:].T
            v_turned[:, n_pre:] = kv_ref[:, HEAD_DIM:].T

        scores = mm(k_all[...], q_ref[...], (1, 1)) * SCORE_SCALE
        scores = jnp.where(allowed_ref[...] != 0, scores, NEGATIVE)
        exp_scores = jnp.exp(scores - jnp.max(scores, axis=0, keepdims=True))
        soft = exp_scores / jnp.sum(exp_scores, axis=0, keepdims=True)
        out_ref[...] = mm(v_turned[...], soft.astype(bf16), (1, 0)).T.astype(bf16)

    return pl.pallas_call(
        kernel,
        out_shape=jax.ShapeDtypeStruct((tokens, QUERY_WIDTH), bf16),
        grid=(HEADS,),
        in_specs=[
            pl.BlockSpec((tokens, HEAD_DIM), lambda h: (0, h)),
            pl.BlockSpec((tokens, 2 * HEAD_DIM), lambda h: (0, HEADS // 2)),
            pl.BlockSpec((n_pre, 2 * HEAD_DIM), lambda h: (0, 0)),
            pl.BlockSpec((keys, tokens), lambda h: (0, 0)),
        ],
        out_specs=pl.BlockSpec((tokens, HEAD_DIM), lambda h: (0, h)),
        scratch_shapes=[pltpu.VMEM((keys, HEAD_DIM), bf16), pltpu.VMEM((HEAD_DIM, keys), bf16)],
        compiler_params=pltpu.CompilerParams(vmem_limit_bytes=VMEM_LIMIT),
        cost_estimate=BRIEF,
        name="attention",
    )(action_qkv, action_qkv, prefix_kv, allowed)


def attention_back(action_qkv, prefix_kv, allowed, back_mixed, first, heads, before):
    tokens, keys = action_qkv.shape[0], allowed.shape[0]
    n_pre = prefix_kv.shape[0]
    last = first + heads == HEADS
    n_before = len(before)

    def kernel(q_ref, kv_ref, pre_ref, allowed_ref, back_ref, *refs):
        before_refs, refs = refs[:n_before], refs[n_before:]
        if last:
            qkv_out, pre_out, k_sum, v_sum, k_all, v_all, k_turned = refs
        else:
            qkv_out, k_sum, v_sum, k_all, v_all, k_turned = refs
        h = pl.program_id(0)

        @pl.when(h == 0)
        def _():
            k_all[:n_pre] = pre_ref[:, :HEAD_DIM]
            k_all[n_pre:] = kv_ref[:, :HEAD_DIM]
            v_all[:n_pre] = pre_ref[:, HEAD_DIM:]
            v_all[n_pre:] = kv_ref[:, HEAD_DIM:]
            k_turned[...] = k_all[...].T
            if n_before:
                qkv_out[:, : first * HEAD_DIM] = before_refs[0][...]
                k_sum[...] = before_refs[1][...]
                v_sum[...] = before_refs[2][...]
            else:
                k_sum[...] = jnp.zeros_like(k_sum)
                v_sum[...] = jnp.zeros_like(v_sum)

        query, back = q_ref[...], back_ref[...]
        scores = mm(k_all[...], query, (1, 1)) * SCORE_SCALE
        scores = jnp.where(allowed_ref[...] != 0, scores, NEGATIVE)
        exp_scores = jnp.exp(scores - jnp.max(scores, axis=0, keepdims=True))
        soft = exp_scores / jnp.sum(exp_scores, axis=0, keepdims=True)
        v_sum[...] += mm(soft.astype(bf16), back, (1, 0))
        back_soft = mm(v_all[...], back, (1, 1))
        mean = jnp.sum(soft * back_soft, axis=0, keepdims=True)
        back_scores = (soft * (back_soft - mean)).astype(bf16)
        k_sum[...] += mm(back_scores, query, (1, 0))
        turned = mm(k_turned[...], back_scores, (1, 0)) * SCORE_SCALE
        at = pl.ds(pl.multiple_of((first + h) * HEAD_DIM, HEAD_DIM), HEAD_DIM)
        qkv_out[:, at] = turned.T.astype(bf16)

        if last:

            @pl.when(h == heads - 1)
            def _():
                pre_out[:, :HEAD_DIM] = (k_sum[:n_pre] * SCORE_SCALE).astype(bf16)
                pre_out[:, HEAD_DIM:] = v_sum[:n_pre].astype(bf16)
                keys_out = (k_sum[n_pre:] * SCORE_SCALE).astype(bf16)
                qkv_out[:, QUERY_WIDTH : QUERY_WIDTH + HEAD_DIM] = keys_out
                qkv_out[:, QUERY_WIDTH + HEAD_DIM :] = v_sum[n_pre:].astype(bf16)

    def once(shape):
        return pl.BlockSpec(shape, lambda h: (0, 0))

    sums = jax.ShapeDtypeStruct((keys, HEAD_DIM), f32)
    if last:
        out_shapes = [
            jax.ShapeDtypeStruct((tokens, QKV_WIDTH), bf16),
            jax.ShapeDtypeStruct((n_pre, 2 * HEAD_DIM), bf16),
        ]
        kept = [pltpu.VMEM(sums.shape, f32)] * 2
    else:
        out_shapes = [jax.ShapeDtypeStruct((tokens, heads * HEAD_DIM), bf16), sums, sums]
        kept = []
    return pl.pallas_call(
        kernel,
        out_shape=out_shapes,
        grid=(heads,),
        in_specs=[
            pl.BlockSpec((tokens, HEAD_DIM), lambda h: (0, first + h)),
            pl.BlockSpec((tokens, 2 * HEAD_DIM), lambda h: (0, HEADS // 2)),
            once((n_pre, 2 * HEAD_DIM)),
            once((keys, tokens)),
            pl.BlockSpec((tokens, HEAD_DIM), lambda h: (0, first + h)),
        ]
        + [once(v.shape) for v in before],
        out_specs=[once(o.shape) for o in out_shapes],
        scratch_shapes=kept
        + [
            pltpu.VMEM((keys, HEAD_DIM), bf16),
            pltpu.VMEM((keys, HEAD_DIM), bf16),
            pltpu.VMEM((HEAD_DIM, keys), bf16),
        ],
        compiler_params=pltpu.CompilerParams(vmem_limit_bytes=VMEM_LIMIT),
        cost_estimate=BRIEF,
        name="attention_back",
    )(action_qkv, action_qkv, prefix_kv, allowed, back_mixed, *before)


def mid_back(residual, back_final, back_own, back_oth, gain_row, out_weight):
    tokens, dim = residual.shape

    def kernel(res_ref, fin_ref, own_ref, oth_ref, gain_ref, weight_ref, attn_out, mixed_out, gain_out):
        v = res_ref[...]
        s = lax.rsqrt(jnp.mean(v * v, axis=-1, keepdims=True) + NORM_EPSILON)
        normed = v * s
        back = own_ref[...] + oth_ref[...]
        gain_out[...] = jnp.sum(back * normed, axis=0, keepdims=True)
        scaled = back * (1.0 + gain_ref[...])
        mean = jnp.mean(scaled * normed, axis=-1, keepdims=True)
        attn = (fin_ref[...] + s * (scaled - normed * mean)).astype(bf16)
        attn_out[...] = attn
        mixed_out[...] = mm(attn, weight_ref[...], (1, 0), bf16)

    return pl.pallas_call(
        kernel,
        out_shape=[
            jax.ShapeDtypeStruct((tokens, dim), bf16),
            jax.ShapeDtypeStruct((tokens, QUERY_WIDTH), bf16),
            jax.ShapeDtypeStruct((1, dim), f32),
        ],
        compiler_params=pltpu.CompilerParams(vmem_limit_bytes=VMEM_LIMIT),
        cost_estimate=BRIEF,
        name="mid_back",
    )(residual, back_final, back_own, back_oth, gain_row, out_weight)


def on_device(
    ring,
    prefix_in,
    action_in,
    target,
    valid_mask,
    prefix_ids,
    action_ids,
    action_blocks,
    learning_rate,
    prefix_weight,
    attention_weight,
    feedforward_weight,
    prefix_gains,
    action_gains,
    readout_weight,
    prefix_weight_moment,
    attention_weight_moment,
    feedforward_weight_moment,
    prefix_gains_moment,
    action_gains_moment,
    readout_weight_moment,
    prefix_weight_average,
    attention_weight_average,
    feedforward_weight_average,
    prefix_gains_average,
    action_gains_average,
    readout_weight_average,
):
    core = lax.axis_index("wide") % 2
    rows_a, width_a = attention_weight.shape
    width_p = 2 * prefix_weight.shape[1]
    rows_p = prefix_weight.shape[0]
    n_right, n_left = ring.n_right, ring.n_left
    order, swap = Order(), ring.to_core

    def by_core(v, size):
        cut = v.reshape(v.shape[0], ring.chips, 2, size)
        cut = [cut[:, :, c].reshape(v.shape[0], ring.chips * size) for c in (0, 1)]
        return jnp.where(core == 0, cut[0], cut[1]), jnp.where(core == 0, cut[1], cut[0])

    def in_order(mine, other, size):
        cut = [jnp.where(core == c, mine, other).reshape(-1, ring.chips, size) for c in (0, 1)]
        return jnp.stack(cut, 2).reshape(mine.shape[0], -1)

    prefix_bf = prefix_weight.astype(bf16)
    packed = jnp.concatenate(
        [attention_weight.astype(bf16), prefix_bf[:rows_a], prefix_bf[rows_a:]], axis=1
    )
    packed = order(packed)
    att = Gathering(ring, order, 0, True)
    att.start("right", packed)
    att.start("left", packed)
    ff_own = order(jnp.transpose(feedforward_weight, (1, 0, 2)).astype(bf16))
    prefix_rows = order(prefix_in[0])
    if rows_p % 128 == 0:
        halves = norm_by_core(ring, prefix_rows, prefix_gains, rows_p)
    else:
        halves = by_core(rms_norm(prefix_rows.astype(f32), prefix_gains[0]).astype(bf16), rows_p)
    pre_mine, pre_other = order(*halves)
    att.step("right", "left")
    action_rows = order(action_in[0]).astype(f32)
    action_norm = rms_norm(action_rows, action_gains[0]).astype(bf16)
    norm_mine, norm_other = order(*by_core(action_norm, rows_a))
    norm_oth = swap(norm_other)
    att.step("right", "left")
    att.settle(("right", 0), ("left", 0))
    ff = Gathering(ring, order, 1, False)
    while att.d["left"] < n_left:
        att.step("left", "right")
    ff.start("left", order(ff_own))
    while att.d["right"] < n_right:
        att.step("right")
    ff.start("right", order(ff_own))
    allowed = order(visible(prefix_ids[0], *order(action_ids[0], action_blocks[0])))
    norm_rows = order(jnp.concatenate([norm_mine, order(norm_oth)], 0))
    sides = [("right", d) for d in range(n_right)] + [("left", d) for d in range(n_left)]
    by_step = sorted(sides, key=lambda k: k[1])
    att.settle(*by_step[:-1])
    ff.step("right")
    att.settle(by_step[-1])
    ff.step("left")
    whole = repack(
        ring, [(packed,)] + [att.blocks[k] for k in sides], None, rows_a, width_a, width_p
    )
    qkv_own, out_own, pre_own = order(*whole)
    pre_oth, qkv_oth, out_oth = swap(pre_own), swap(qkv_own), swap(out_own)

    pre_oth, qkv_oth = order(pre_oth, qkv_oth)
    prefix_kv = (mm(pre_mine, pre_own, (1, 0)) + mm(pre_other, pre_oth, (1, 0))).astype(bf16)
    action_qkv = (mm(norm_mine, qkv_own, (1, 0)) + mm(norm_other, qkv_oth, (1, 0))).astype(bf16)
    prefix_kv, action_qkv = order(prefix_kv, action_qkv)
    ff.step("right")
    out_own, out_oth = order(out_own, out_oth)
    out_weight = order(interleave(ring, out_own, out_oth, rows_a))
    action_qkv = order(action_qkv)
    mixed_heads = order(attention(action_qkv, prefix_kv, allowed))
    mixed_oth = swap(mixed_heads)
    ff.step("right", "left")
    mixed_heads = order(mixed_heads)
    residual = action_rows + mm(mixed_heads, out_weight, (1, 1))
    tokens = residual.shape[0]
    hidden_norm = rms_norm(residual, action_gains[1]).astype(bf16)
    residual, hidden_norm = order(residual, hidden_norm)
    norm_two = order(jnp.concatenate([hidden_norm, swap(hidden_norm)], 0))

    def weights(key):
        return (ff_own,) if key[0] == "own" else ff.blocks[key]

    early = [("own", 0)] + [x for d in range(n_left - 1) for x in (("left", d), ("right", d))]
    late = [("right", n_left - 1), ("left", n_left - 1)]
    late += [("right", d) for d in range(n_left, n_right)]
    groups = [early, late]
    while ff.d["left"] < n_left - 1:
        ff.step("left", "right")
    kept, branch = [], None
    for group in groups:
        while any(k[0] != "own" and k not in ff.blocks for k in group):
            ff.step("right", "left")
        ff.settle(*group)
        norm_two = order(norm_two)
        *values, own_rows, other_rows = ff_forward(norm_two, [weights(k) for k in group], branch)
        branch = order(own_rows, other_rows)
        kept.append(values)
    final_stream = residual + branch[0] + swap(branch[1])
    final_norm = rms_norm(final_stream, action_gains[2])
    predicted = jnp.dot(final_norm, readout_weight, precision=HIGHEST)
    valid_rows = valid_mask[0].astype(f32)
    error_term = predicted - target[0]

    loss_sum = jnp.sum(valid_rows * error_term * error_term)
    own_count = jnp.sum(valid_rows)
    back_predicted = 2.0 * valid_rows * error_term
    back_final, grad_gain_final = norm_back(
        final_stream, action_gains[2], jnp.dot(back_predicted, readout_weight.T, precision=HIGHEST)
    )
    back_branch = back_final.astype(bf16)
    back_final, back_branch = order(back_final, back_branch)
    branch_two = order(jnp.concatenate([back_branch, swap(back_branch)], 0))
    ff_sum = Summing(ring, order, 1)
    grads, back = {}, None
    for group, values in zip(reversed(groups), reversed(kept)):
        turned = group[::-1]
        branch_two = order(branch_two)
        made, back = ff_backward(
            norm_two, branch_two, [weights(k) for k in turned], values, (len(group) - 1, -1), back
        )
        flat = order(*back, *[p for parts in made for p in parts])
        back, flat = flat[:2], list(flat[2:])
        for k, parts in zip(turned, made):
            grads[k] = tuple(flat.pop(0) for _ in parts)
            if k[0] != "own":
                ff_sum.put(k, grads[k])
        if group is late:
            ff_sum.step("left")
    back_oth = swap(back[1])
    ff_sum.step("right")
    back_own, back_oth = order(back[0], back_oth)
    back_attention, back_mixed, grad_gain_hidden = order(
        *mid_back(residual, back_final, back_own, back_oth, action_gains[1:2], out_weight)
    )
    part = order(
        *attention_back(action_qkv, prefix_kv, allowed, back_mixed, 0, HEADS // 2, ())
    )
    ff_sum.step("left")
    ff_sum.step("right")
    back_mixed, *part = order(back_mixed, *part)
    back_qkv, back_prefix_kv = order(
        *attention_back(action_qkv, prefix_kv, allowed, back_mixed, HEADS // 2, HEADS // 2, part)
    )
    qkv_back_oth = swap(back_qkv)

    attn_mine, attn_other = order(*by_core(order(back_attention), rows_a))
    attn_oth = swap(attn_other)
    other_side = order(mm(pre_other, order(back_prefix_kv), (0, 0), bf16))
    other_side = swap(other_side)
    attn_oth, mixed_oth = order(attn_oth, mixed_oth)
    grad_output = order(
        mm(
            jnp.concatenate([attn_mine, attn_oth], 0),
            jnp.concatenate([mixed_heads, mixed_oth], 0),
            (0, 0),
            bf16,
        )
    )
    ff_sum.step("right")
    qkv_back_oth = order(qkv_back_oth)
    grad_qkv = order(mm(norm_rows, jnp.concatenate([back_qkv, qkv_back_oth], 0), (0, 0), bf16))
    other_side = order(other_side)
    prefix_sum = mm(pre_mine, back_prefix_kv, (0, 0)) + other_side.astype(f32)
    prefix_sum = order(prefix_sum.astype(bf16))
    ff_sum.step("left")
    cut = repack(
        ring,
        [1] + [len(att.blocks[k]) for k in sides],
        [grad_qkv, grad_output, prefix_sum],
        rows_a,
        width_a,
        width_p,
    )
    flat = list(order(*[p for parts in cut for p in parts]))
    cut = [tuple(flat.pop(0) for _ in parts) for parts in cut]
    own_cut, cut = cut[0][0], dict(zip(sides, cut[1:]))
    att_sum = Summing(ring, order, 0)
    far_first = sorted(sides, key=lambda k: (-k[1], k[0] == "left"))
    for k in far_first:
        att_sum.put(k, cut[k])
    split_left = len(cut["left", 0]) == 2
    if split_left:
        att_sum.own(own_cut)
    ff_sum.step("right")

    def gain_gradient(mine, other, size, gain_row):
        sums = [jnp.sum(m, axis=0, keepdims=True) for m in (mine, other)]
        return in_order(*sums, size)[0] / (1.0 + gain_row)

    back_qkv, back_prefix_kv = order(back_qkv, back_prefix_kv)
    grad_gain_action = gain_gradient(
        mm(back_qkv, qkv_own, (1, 1)) * norm_mine.astype(f32),
        mm(back_qkv, qkv_oth, (1, 1)) * norm_other.astype(f32),
        rows_a,
        action_gains[0],
    )
    grad_gain_prefix = gain_gradient(
        mm(back_prefix_kv, pre_own, (1, 1)) * pre_mine.astype(f32),
        mm(back_prefix_kv, pre_oth, (1, 1)) * pre_other.astype(f32),
        rows_p,
        prefix_gains[0],
    )
    back_predicted, final_norm = order(back_predicted, final_norm)
    grad_readout = lax.dot_general(
        back_predicted, final_norm, (((0,), (0,)), ((), ())), precision=HIGHEST
    )
    dim = action_rows.shape[1]
    small = order(
        jnp.concatenate(
            [
                grad_readout,
                grad_gain_prefix.reshape(-1, dim),
                grad_gain_action[None],
                grad_gain_hidden,
                grad_gain_final[None],
                jnp.full((1, dim), loss_sum),
                jnp.full((1, dim), own_count),
            ],
            0,
        )
    )
    while ff_sum.left():
        ff_sum.step("right", "left")
    steps = ring.bits()
    moved = steps.pop(0)(small)
    for i, key in enumerate(far_first):
        att_sum.ready(key, *far_first[i + 1 : i + 2])
        if i == 0:
            ff_sum.land("right")
        att_sum.step(key[0])
        if i == 1:
            ff_sum.own(grads["own", 0][0])
        if moved is not None:
            small, moved = order(small, moved)
            small = order(small + moved)
            moved = steps.pop(0)(small) if steps else None
        if i == 3:
            ff_sum.close()
    while moved is not None:
        small, moved = order(small, moved)
        small = order(small + moved)
        moved = steps.pop(0)(small) if steps else None
    if not split_left:
        att_sum.own(own_cut)
    ff_total = ff_sum.result()
    act = grad_readout.shape[0]
    n_pre = grad_gain_prefix.shape[0] // dim
    count = small[act + n_pre + 4, 0]
    loss_value = small[act + n_pre + 3, 0] / count
    scale = 1.0 / count
    step_rate = learning_rate[0]
    third = order(
        *advance(
            feedforward_weight,
            feedforward_weight_moment,
            feedforward_weight_average,
            jnp.transpose(ff_total, (1, 0, 2)) * scale,
            step_rate,
        )
    )
    att_sum.close()
    packed_total = att_sum.result()
    first = advance(
        prefix_weight,
        prefix_weight_moment,
        prefix_weight_average,
        jnp.concatenate(
            [
                packed_total[:, width_a : width_a + width_p // 2],
                packed_total[:, width_a + width_p // 2 :],
            ],
            0,
        )
        * scale,
        step_rate,
    )
    second = advance(
        attention_weight,
        attention_weight_moment,
        attention_weight_average,
        packed_total[:, :width_a] * scale,
        step_rate,
    )
    fourth = advance(
        prefix_gains,
        prefix_gains_moment,
        prefix_gains_average,
        small[act : act + n_pre].reshape(1, -1) * scale,
        step_rate,
    )
    fifth = advance(
        action_gains,
        action_gains_moment,
        action_gains_average,
        small[act + n_pre : act + n_pre + 3] * scale,
        step_rate,
    )
    sixth = advance(
        readout_weight,
        readout_weight_moment,
        readout_weight_average,
        small[:act].T * scale,
        step_rate,
    )
    return (loss_value,) + tuple(
        group[i]
        for i in range(3)
        for group in (first, second, third, fourth, fifth, sixth)
    )


def solution(mesh):
    rows = P(("batch", "wide"))
    wide = P("wide")
    whole = P()
    weights = (wide, wide, wide, whole, whole, whole)
    return jax.shard_map(
        functools.partial(on_device, Ring(mesh.shape["wide"])),
        mesh=mesh,
        in_specs=(rows,) * 7 + (whole,) + weights * 3,
        out_specs=(whole,) + weights * 3,
        check_vma=False,
    )
```

time: 617 us -> 477 us (0.77)
  waiting for transfers between devices: 302 us -> 180 us
  local copies, waits for them, and re-layouts: 43.1 us -> 26 us
  Pallas kernels: 93.1 us -> 110 us
  between operations: 20 us -> 6.16 us
  starting transfers between devices: 74.7 us -> 66.3 us
    ppermute x14, waiting for transfers between devices: 118 us -> 21.3 us  [to_right(): return lax.ppermute(v, 'wide', self.right)]
    pallas_call x2 -> x7, Pallas kernels: 30 us -> 47.9 us  [the longest x2 23.2 us: attention_back(): pl.pallas_call(kernel, out_shape=out_shapes, grid=(heads,), in_specs=[pl....]
    ppermute x14, waiting for transfers between devices: 54.4 us -> 40.6 us  [to_left(): return lax.ppermute(v, 'wide', self.left)]
    convert_element_type x21 -> x20, other arithmetic: 16.2 us -> 29.5 us  [the longest x16 23.7 us: add(): return sum((t.astype(f32) for t in terms)).astype(bf16)]
    ppermute x21 -> x27, waiting for transfers between devices: 115 us -> 102 us  [to_peer(): return lax.ppermute(v, 'batch', [(0, 1), (1, 0)])]
    reshape x3 -> x0, local copies, waits for them, and re-layouts: 7.92 us -> none  [the longest x1 4.42 us: on_device(): grad_prefix = grad_prefix.reshape(2, ring.chips * rows_a, 2 * width_p)]
    ppermute x14, starting transfers between devices: 18.5 us -> 11.2 us  [to_right(): return lax.ppermute(v, 'wide', self.right)]
    unnamed x191 -> x183, local copies, waits for them, and re-layouts: 17.3 us -> 14 us
  transfers between devices with their start and end apart: 74 -> 71, of which waited for: 30 -> 36; matrix products, arithmetic and copies ran while one was open for 15% -> 17% of each run, Pallas kernels for 8% -> 19%
where the time goes in v2:
time: 477 us; the launch traced here: 468 us
  waiting for transfers between devices  180 us (38%)
  Pallas kernels  110 us (23%)
  starting transfers between devices  66.3 us (14%)
  other arithmetic  48.5 us (10%)
  matrix products  30.5 us (6%)
  local copies, waits for them, and re-layouts  26 us (5%)
  between operations  6.16 us (1%)
    ppermute x27, waiting for transfers between devices, to_peer(): return lax.ppermute(v, 'batch', [(0, 1), (1, 0)])  102 us
    ppermute x14, waiting for transfers between devices, to_left(): return lax.ppermute(v, 'wide', self.left)  40.6 us
    pallas_call x2, Pallas kernels, ff_backward(): pl.pallas_call(kernel, out_shape=[jax.ShapeDtypeStruct(a.shape, bf16) for...  32.9 us
    ppermute x27, starting transfers between devices, to_peer(): return lax.ppermute(v, 'batch', [(0, 1), (1, 0)])  27.9 us
    dot_general x13, matrix products, mm(): lax.dot_general(a, b, (((contract[0],), (contract[1],)), ((), ())), prefe...  25.1 us
    convert_element_type x16, other arithmetic, add(): return sum((t.astype(f32) for t in terms)).astype(bf16)  23.7 us
    pallas_call x2, Pallas kernels, attention_back(): pl.pallas_call(kernel, out_shape=out_shapes, grid=(heads,), in_specs=[pl....  23.2 us
    ppermute x14, waiting for transfers between devices, to_right(): return lax.ppermute(v, 'wide', self.right)  21.3 us
  transfers between devices with their start and end apart: 71, of which 36 were waited for; matrix products, arithmetic and copies ran while one was open for 17% of the time, Pallas kernels for 19%

profile of v2, /device:TPU:0, one launch (start us, length us, event | category | flops | bytes accessed | tf_op | source)
XLA Modules:
  0.0 467.7 jit_solution(11239990023955944887)
XLA Ops:
  9.5 6.0 %norm_by_core.1 = (bf16[1024,1024]{1,0:T(8,128)(2,1)S(1)}, bf16[1024,1024]{1,0:T(8,128)(2,1)S(1)}) custom-call(s32[1]{0:T(128)} %bitcast.2.core_ref, bf16[1024,2048]{1,0:T(8,128)(2,1)} %bitcast.89, f32[1,2048]{1,0:T(1,128)S(1)} %copy-done.29), custom_call_target="tpu_custom_call" | custom-call | flops 1 | bytes 1 | tf_op jit(solution)/shard_map/norm_by_core/pallas_call | solution.py:357
  32.9 4.5 collective-permute-done.8.refs_2_
  45.1 5.1 %collective-permute-done.9.refs_7_ = bf16[32,5632]{1,0:T(8,128)(2,1)} collective-permute-done((bf16[32,5632]{1,0:T(8,128)(2,1)}, bf16[32,5632]{1,0:T(8,128)(2,1)}, u32[]{:S(2)}, u32[]{:S(2)}) %collective-permute-start.9) | collective-permute-done | bytes 360480 | tf_op jit(solution)/shard_map/ppermute | solution.py:94
  54.8 7.2 %collective-permute-done.11.refs_12_ = bf16[32,5632]{1,0:T(8,128)(2,1)S(1)} collective-permute-done((bf16[32,5632]{1,0:T(8,128)(2,1)S(1)}, bf16[32,5632]{1,0:T(8,128)(2,1)S(1)}, u32[]{:S(2)}, u32[]{:S(2)}) %collective-permute-start.11) | collective-permute-done | bytes 360480 | tf_op jit(solution)/shard_map/ppermute | solution.py:103
  63.5 6.2 %collective-permute-done.12.refs_6_ = bf16[32,5632]{1,0:T(8,128)(2,1)S(1)} collective-permute-done((bf16[32,5632]{1,0:T(8,128)(2,1)}, bf16[32,5632]{1,0:T(8,128)(2,1)S(1)}, u32[]{:S(2)}, u32[]{:S(2)}) %collective-permute-start.12) | collective-permute-done | bytes 360480 | tf_op jit(solution)/shard_map/ppermute | solution.py:103
  69.7 7.7 %collective-permute-done.14.refs_14_ = bf16[32,5632]{1,0:T(8,128)(2,1)S(1)} collective-permute-done((bf16[32,5632]{1,0:T(8,128)(2,1)}, bf16[32,5632]{1,0:T(8,128)(2,1)S(1)}, u32[]{:S(2)}, u32[]{:S(2)}) %collective-permute-start.14) | collective-permute-done | bytes 360480 | tf_op jit(solution)/shard_map/ppermute | solution.py:103
  77.4 7.3 %collective-permute-done.15.refs_8_ = bf16[32,5632]{1,0:T(8,128)(2,1)S(1)} collective-permute-done((bf16[32,5632]{1,0:T(8,128)(2,1)}, bf16[32,5632]{1,0:T(8,128)(2,1)S(1)}, u32[]{:S(2)}, u32[]{:S(2)}) %collective-permute-start.15) | collective-permute-done | bytes 360480 | tf_op jit(solution)/shard_map/ppermute | solution.py:103
  84.8 6.3 %assemble.1 = (bf16[512,2560]{1,0:T(8,128)(2,1)}, bf16[512,2048]{1,0:T(8,128)(2,1)}, bf16[1024,512]{1,0:T(8,128)(2,1)}) custom-call(s32[2,15]{1,0:T(2,128)S(1)} %fusion.22.table_ref, bf16[64,5632]{1,0:T(8,128)(2,1)S(1)} %pad_maximum_fusion.2.refs_0_, bf16[32,5632]{1,0:T(8,128)(2,1)S(1)} %collective-permute-done.1.refs_1_, bf16[32,5632]{1,0:T(8,128)(2,1)S(1)} %copy-done.28, ...), custom_call_target="tpu_custom_call" | custom-call | flops 1 | bytes 1 | tf_op jit(solution)/shard_map/assemble/pallas_call | solution.py:283
  101.6 9.6 %collective-permute-done.20.refs_5_.refs_0_ = bf16[3,128,1024]{2,1,0:T(8,128)(2,1)S(1)} collective-permute-done((bf16[3,128,1024]{2,1,0:T(8,128)(2,1)S(1)}, bf16[3,128,1024]{2,1,0:T(8,128)(2,1)S(1)}, u32[]{:S(2)}, u32[]{:S(2)}) %collective-permute-start.20) | collective-permute-done | bytes 786464 | tf_op jit(solution)/shard_map/ppermute | solution.py:94
  116.3 12.5 %attention.1 = bf16[256,2048]{1,0:T(8,128)(2,1)S(1)} custom-call(bf16[256,2560]{1,0:T(8,128)(2,1)S(1)} %fusion.q_ref.kv_ref, bf16[256,2560]{1,0:T(8,128)(2,1)S(1)} %fusion.q_ref.kv_ref, bf16[1024,512]{1,0:T(8,128)(2,1)S(1)} %add_convert_fusion.4.pre_ref, s32[1280,256]{1,0:T(8,128)S(1)} %add_convert_fusion.10.allowed_ref), custom_call_target="tpu_custom_call" | custom-call | flops 1 | bytes 1 | tf_op jit(solution)/shard_map/attention/pallas_call | solution.py:591
  141.8 7.2 %collective-permute-done.24.refs_6_.refs_1_ = bf16[3,128,1024]{2,1,0:T(8,128)(2,1)S(1)} collective-permute-done((bf16[3,128,1024]{2,1,0:T(8,128)(2,1)S(1)}, bf16[3,128,1024]{2,1,0:T(8,128)(2,1)S(1)}, u32[]{:S(2)}, u32[]{:S(2)}) %collective-permute-start.24) | collective-permute-done | bytes 786464 | tf_op jit(solution)/shard_map/ppermute | solution.py:103
  149.0 9.6 %ff_forward.2 = (f32[5,512,256]{2,1,0:T(8,128)}, f32[5,512,256]{2,1,0:T(8,128)}, bf16[5,512,256]{2,1,0:T(8,128)(2,1)}, f32[256,1024]{1,0:T(8,128)S(1)}, f32[256,1024]{1,0:T(8,128)S(1)}) custom-call(bf16[512,1024]{1,0:T(8,128)(2,1)} %pad_maximum_fusion.norm_ref, bf16[3,256,1024]{2,1,0:T(8,128)(2,1)} %convert_bitcast_fusion.refs_0_.refs_6_, ...), custom_call_target="tpu_custom_call" | custom-call | flops 1 | bytes 1 | tf_op jit(solution)/shard_map/ff_forward/pallas_call | solution.py:448
  161.1 11.4 %collective-permute-done.28.refs_2_ = bf16[3,256,1024]{2,1,0:T(8,128)(2,1)S(1)} collective-permute-done((bf16[3,256,1024]{2,1,0:T(8,128)(2,1)}, bf16[3,256,1024]{2,1,0:T(8,128)(2,1)S(1)}, u32[]{:S(2)}, u32[]{:S(2)}) %collective-permute-start.28) | collective-permute-done | bytes 1572896 | tf_op jit(solution)/shard_map/ppermute | solution.py:97
  172.5 8.2 %collective-permute-done.27.refs_4_.refs_1_ = bf16[3,128,1024]{2,1,0:T(8,128)(2,1)S(1)} collective-permute-done((bf16[3,128,1024]{2,1,0:T(8,128)(2,1)S(1)}, bf16[3,128,1024]{2,1,0:T(8,128)(2,1)S(1)}, u32[]{:S(2)}, u32[]{:S(2)}) %collective-permute-start.27) | collective-permute-done | bytes 786464 | tf_op jit(solution)/shard_map/ppermute | solution.py:103
  180.8 7.1 %ff_forward.3 = (f32[3,512,256]{2,1,0:T(8,128)}, f32[3,512,256]{2,1,0:T(8,128)}, bf16[3,512,256]{2,1,0:T(8,128)(2,1)S(1)}, f32[256,1024]{1,0:T(8,128)S(1)}, f32[256,1024]{1,0:T(8,128)S(1)}) custom-call(bf16[512,1024]{1,0:T(8,128)(2,1)} %pad_maximum_fusion.norm_ref, bf16[3,128,1024]{2,1,0:T(8,128)(2,1)S(1)} %collective-permute-done.22.refs_0_.refs_3_, ...), custom_call_target="tpu_custom_call" | custom-call | flops 1 | bytes 1 | tf_op jit(solution)/shard_map/ff_forward/pallas_call | solution.py:448
  198.6 13.1 %ff_backward.2 = (bf16[3,128,1024]{2,1,0:T(8,128)(2,1)S(1)}, bf16[3,128,1024]{2,1,0:T(8,128)(2,1)S(1)}, bf16[3,256,1024]{2,1,0:T(8,128)(2,1)}, bf16[3,128,1024]{...) custom-call(bf16[512,1024]{1,0:T(8,128)(2,1)} %pad_maximum_fusion.norm_ref, ...), custom_call_target="tpu_custom_call" | custom-call | flops 1 | bytes 1 | tf_op jit(solution)/shard_map/ff_backward/pallas_call | solution.py:550
  213.8 19.9 %ff_backward.3 = (bf16[3,128,1024]{2,1,0:T(8,128)(2,1)S(1)}, bf16[3,128,1024]{2,1,0:T(8,128)(2,1)S(1)}, bf16[3,256,1024]{2,1,0:T(8,128)(2,1)}, bf16[3,128,1024]{...) custom-call(bf16[512,1024]{1,0:T(8,128)(2,1)} %pad_maximum_fusion.no, ...), custom_call_target="tpu_custom_call" | custom-call | flops 1 | bytes 1 | tf_op jit(solution)/shard_map/ff_backward/pallas_call | solution.py:550
  249.9 11.2 %attention_back.2 = (bf16[256,1024]{1,0:T(8,128)(2,1)S(1)}, f32[1280,256]{1,0:T(8,128)S(1)}, f32[1280,256]{1,0:T(8,128)S(1)}) custom-call(bf16[256,2560]{1,0:T(8,128)(2,1)} %copy-done, bf16[256,2560]{1,0:T(8,128)(2,1)} %copy-done, bf16[1024,512]{1,0:T(8,128)(2,1)S(1)} %copy-done.3, s32[1280,256]{1,0:T(8,128)} %copy-done.1, ...), custom_call_target="tpu_custom_call" | custom-call | flops 1 | bytes 1 | tf_op jit(solution)/shard_map/attention_back/pallas_call | solution.py:675
  268.6 12.0 %attention_back.3 = (bf16[256,2560]{1,0:T(8,128)(2,1)S(1)}, bf16[1024,512]{1,0:T(8,128)(2,1)S(1)}) custom-call(bf16[256,2560]{1,0:T(8,128)(2,1)} %copy-done, bf16[256,2560]{1,0:T(8,128)(2,1)} %copy-done, bf16[1024,512]{1,0:T(8,128)(2,1)S(1)} %copy-done.3, s32[1280,256]{1,0:T(8,128)} %copy-done.1, bf16[256,2048]{1,0:T(8,128)(2,1)S(1)} %get-tuple-element.681.back_ref, ...), custom_call_target="tpu_custom_call" | custom-call | flops 1 | bytes 1 | tf_op jit(solution)/shard_map/attention_back/pallas_call | solution.py:675
  293.9 7.6 %collective-permute-done.39 = bf16[3,128,1024]{2,1,0:T(8,128)(2,1)} collective-permute-done((bf16[3,128,1024]{2,1,0:T(8,128)(2,1)}, bf16[3,128,1024]{2,1,0:T(8,128)(2,1)}, u32[]{:S(2)}, u32[]{:S(2)}) %collective-permute-start.39) | collective-permute-done | bytes 786464 | tf_op jit(solution)/shard_map/ppermute | solution.py:97
  309.1 5.4 %disassemble.1 = (bf16[64,5632]{1,0:T(8,128)(2,1)S(1)}, bf16[32,5632]{1,0:T(8,128)(2,1)S(1)}, bf16[32,5632]{1,0:T(8,128)(2,1)}, bf16[32,5632]{1,0:T(8,128)(2,1)S...) custom-call(s32[2,15]{1,0:T(2,128)S(1)} %fusion.22.table_ref, ...), custom_call_target="tpu_custom_call" | custom-call | flops 1 | bytes 1 | tf_op jit(solution)/shard_map/disassemble/pallas_call | solution.py:283
  346.7 7.0 %collective-permute-done.55 = bf16[32,5632]{1,0:T(8,128)(2,1)} collective-permute-done((bf16[32,5632]{1,0:T(8,128)(2,1)}, bf16[32,5632]{1,0:T(8,128)(2,1)}, u32[]{:S(2)}, u32[]{:S(2)}) %collective-permute-start.55) | collective-permute-done | bytes 360480 | tf_op jit(solution)/shard_map/ppermute | solution.py:103
  355.3 6.2 %collective-permute-done.64 = bf16[32,5632]{1,0:T(8,128)(2,1)} collective-permute-done((bf16[32,5632]{1,0:T(8,128)(2,1)}, bf16[32,5632]{1,0:T(8,128)(2,1)}, u32[]{:S(2)}, u32[]{:S(2)}) %collective-permute-start.64) | collective-permute-done | bytes 360480 | tf_op jit(solution)/shard_map/ppermute | solution.py:103
  363.0 6.2 %collective-permute-done.58 = bf16[32,5632]{1,0:T(8,128)(2,1)} collective-permute-done((bf16[32,5632]{1,0:T(8,128)(2,1)S(1)}, bf16[32,5632]{1,0:T(8,128)(2,1)}, u32[]{:S(2)}, u32[]{:S(2)}) %collective-permute-start.58) | collective-permute-done | bytes 360480 | tf_op jit(solution)/shard_map/ppermute | solution.py:103
  371.8 14.1 %collective-permute-done.46 = f32[39,1024]{1,0:T(8,128)S(1)} collective-permute-done((f32[39,1024]{1,0:T(8,128)S(1)}, f32[39,1024]{1,0:T(8,128)S(1)}, u32[]{:S(2)}, u32[]{:S(2)}) %collective-permute-start.46) | collective-permute-done | bytes 159776 | tf_op jit(solution)/shard_map/ppermute | solution.py:103
  388.2 8.6 %collective-permute-done.52 = bf16[32,5632]{1,0:T(8,128)(2,1)S(1)} collective-permute-done((bf16[32,5632]{1,0:T(8,128)(2,1)S(1)}, bf16[32,5632]{1,0:T(8,128)(2,1)S(1)}, u32[]{:S(2)}, u32[]{:S(2)}) %collective-permute-start.52) | collective-permute-done | bytes 360480 | tf_op jit(solution)/shard_map/ppermute | solution.py:97
  401.2 6.8 %collective-permute-done.57 = bf16[32,5632]{1,0:T(8,128)(2,1)S(1)} collective-permute-done((bf16[32,5632]{1,0:T(8,128)(2,1)S(1)}, bf16[32,5632]{1,0:T(8,128)(2,1)S(1)}, u32[]{:S(2)}, u32[]{:S(2)}) %collective-permute-start.57) | collective-permute-done | bytes 360480 | tf_op jit(solution)/shard_map/ppermute | solution.py:97
  424.1 4.4 collective-permute-start.59
  430.0 5.0 %collective-permute-done.59 = f32[39,1024]{1,0:T(8,128)S(1)} collective-permute-done((f32[39,1024]{1,0:T(8,128)S(1)}, f32[39,1024]{1,0:T(8,128)S(1)}, u32[]{:S(2)}, u32[]{:S(2)}) %collective-permute-start.59) | collective-permute-done | bytes 159776 | tf_op jit(solution)/shard_map/ppermute | solution.py:990
  444.2 5.6 %collective-permute-done.69 = bf16[32,5632]{1,0:T(8,128)(2,1)S(1)} collective-permute-done((bf16[32,5632]{1,0:T(8,128)(2,1)S(1)}, bf16[32,5632]{1,0:T(8,128)(2,1)S(1)}, u32[]{:S(2)}, u32[]{:S(2)}) %collective-permute-start.69) | collective-permute-done | bytes 360480 | tf_op jit(solution)/shard_map/ppermute | solution.py:103
  453.1 8.5 %collective-permute-done.70 = bf16[3,128,1024]{2,1,0:T(8,128)(2,1)S(1)} collective-permute-done((bf16[3,128,1024]{2,1,0:T(8,128)(2,1)S(1)}, bf16[3,128,1024]{2,1,0:T(8,128)(2,1)S(1)}, u32[]{:S(2)}, u32[]{:S(2)}) %collective-permute-start.70) | collective-permute-done | bytes 786464 | tf_op jit(solution)/shard_map/ppermute | solution.py:103
  461.6 4.5 multiply_add_fusion
  (403 shorter events, 199.4 us)
Async XLA Ops:
  40.3 50.8 %collective-permute-start.16 = (bf16[3,256,1024]{2,1,0:T(8,128)(2,1)}, bf16[3,256,1024]{2,1,0:T(8,128)(2,1)}, u32[]{:S(2)}, u32[]{:S(2)}) collective-permute-start(bf16[3,256,1024]{2,1,0:T(8,128)(2,1)} %convert_bitcast_fusion.refs_0_.refs_6_), channel_id=1, source_target_pairs={{4,0},{5,1},{8,4},{9,5},{12,8},{13,9},{14,12},{15,13},{10,14},{11,... | collective-permute-start | bytes 4718600 | tf_op jit(solution)/shard_map/ppermute | solution.py:97
  51.4 26.0 %collective-permute-start.13 = (bf16[3,128,1024]{2,1,0:T(8,128)(2,1)S(1)}, bf16[3,128,1024]{2,1,0:T(8,128)(2,1)S(1)}, u32[]{:S(2)}, u32[]{:S(2)}) collective-permute-start(bf16[3,128,1024]{2,1,0:T(8,128)(2,1)S(1)} %constant_dynamic-slice_fusion.3), channel_id=1, source_target_pairs={{0,4},{1,5},{4,8},{5,9},{8,12},{9,13},{12,14},{13,15},{14,10},{15,... | collective-permute-start | bytes 2359304 | tf_op jit(solution)/shard_map/ppermute | solution.py:94
  54.3 23.2 %collective-permute-start.14 = (bf16[32,5632]{1,0:T(8,128)(2,1)}, bf16[32,5632]{1,0:T(8,128)(2,1)S(1)}, u32[]{:S(2)}, u32[]{:S(2)}) collective-permute-start(bf16[32,5632]{1,0:T(8,128)(2,1)} %collective-permute-done.6.refs_13_), channel_id=1, source_target_pairs={{0,16},{16,0},{1,17},{17,1},{2,18},{18,2},{3,19},{19,3},{4,20},{20... | collective-permute-start | bytes 1081352 | tf_op jit(solution)/shard_map/ppermute | solution.py:103
  62.0 22.8 %collective-permute-start.15 = (bf16[32,5632]{1,0:T(8,128)(2,1)}, bf16[32,5632]{1,0:T(8,128)(2,1)S(1)}, u32[]{:S(2)}, u32[]{:S(2)}) collective-permute-start(bf16[32,5632]{1,0:T(8,128)(2,1)} %collective-permute-done.9.refs_7_), channel_id=1, source_target_pairs={{0,16},{16,0},{1,17},{17,1},{2,18},{18,2},{3,19},{19,3},{4,20},{20... | collective-permute-start | bytes 1081352 | tf_op jit(solution)/shard_map/ppermute | solution.py:103
  92.2 21.6 %collective-permute-start.19 = (bf16[512,2048]{1,0:T(8,128)(2,1)}, bf16[512,2048]{1,0:T(8,128)(2,1)S(1)}, u32[]{:S(2)}, u32[]{:S(2)}) collective-permute-start(bf16[512,2048]{1,0:T(8,128)(2,1)} %get-tuple-element.545.own_ref), channel_id=1, source_target_pairs={{0,1},{1,0},{2,3},{3,2},{4,5},{5,4},{6,7},{7,6},{8,9},{9,8},{10,11... | collective-permute-start | bytes 6291464 | tf_op jit(solution)/shard_map/ppermute | solution.py:100
  94.8 37.2 %collective-permute-start.21 = (bf16[3,256,1024]{2,1,0:T(8,128)(2,1)}, bf16[3,256,1024]{2,1,0:T(8,128)(2,1)}, u32[]{:S(2)}, u32[]{:S(2)}) collective-permute-start(bf16[3,256,1024]{2,1,0:T(8,128)(2,1)} %collective-permute-done.16.refs_1_.refs_5_), channel_id=1, source_target_pairs={{4,0},{5,1},{8,4},{9,5},{12,8},{13,9},{14,12},{15,13},{10,14},{11,... | collective-permute-start | bytes 4718600 | tf_op jit(solution)/shard_map/ppermute | solution.py:97
  111.7 30.1 %collective-permute-start.25 = (bf16[3,128,1024]{2,1,0:T(8,128)(2,1)S(1)}, bf16[3,128,1024]{2,1,0:T(8,128)(2,1)S(1)}, u32[]{:S(2)}, u32[]{:S(2)}) collective-permute-start(bf16[3,128,1024]{2,1,0:T(8,128)(2,1)S(1)} %collective-permute-done.13.refs_2_.refs_3_), channel_id=1, source_target_pairs={{0,16},{16,0},{1,17},{17,1},{2,18},{18,2},{3,19},{19,3},{4,20},{20... | collective-permute-start | bytes 2359304 | tf_op jit(solution)/shard_map/ppermute | solution.py:103
  112.2 36.8 %collective-permute-start.24 = (bf16[3,128,1024]{2,1,0:T(8,128)(2,1)S(1)}, bf16[3,128,1024]{2,1,0:T(8,128)(2,1)S(1)}, u32[]{:S(2)}, u32[]{:S(2)}) collective-permute-start(bf16[3,128,1024]{2,1,0:T(8,128)(2,1)S(1)} %collective-permute-done.20.refs_5_.refs_0_), channel_id=1, source_target_pairs={{0,16},{16,0},{1,17},{17,1},{2,18},{18,2},{3,19},{19,3},{4,20},{20... | collective-permute-start | bytes 2359304 | tf_op jit(solution)/shard_map/ppermute | solution.py:103
  135.5 25.0 %collective-permute-start.26 = (bf16[3,128,1024]{2,1,0:T(8,128)(2,1)S(1)}, bf16[3,128,1024]{2,1,0:T(8,128)(2,1)S(1)}, u32[]{:S(2)}, u32[]{:S(2)}) collective-permute-start(bf16[3,128,1024]{2,1,0:T(8,128)(2,1)S(1)} %collective-permute-done.22.refs_0_.refs_3_), channel_id=1, source_target_pairs={{0,4},{1,5},{4,8},{5,9},{8,12},{9,13},{12,14},{13,15},{14,10},{15,... | collective-permute-start | bytes 2359304 | tf_op jit(solution)/shard_map/ppermute | solution.py:94
  136.1 36.4 %collective-permute-start.28 = (bf16[3,256,1024]{2,1,0:T(8,128)(2,1)}, bf16[3,256,1024]{2,1,0:T(8,128)(2,1)S(1)}, u32[]{:S(2)}, u32[]{:S(2)}) collective-permute-start(bf16[3,256,1024]{2,1,0:T(8,128)(2,1)} %collective-permute-done.21.refs_4_.refs_2_), channel_id=1, source_target_pairs={{4,0},{5,1},{8,4},{9,5},{12,8},{13,9},{14,12},{15,13},{10,14},{11,... | collective-permute-start | bytes 4718600 | tf_op jit(solution)/shard_map/ppermute | solution.py:97
  140.2 32.3 %collective-permute-start.29 = (bf16[3,128,1024]{2,1,0:T(8,128)(2,1)S(1)}, bf16[3,128,1024]{2,1,0:T(8,128)(2,1)S(1)}, u32[]{:S(2)}, u32[]{:S(2)}) collective-permute-start(bf16[3,128,1024]{2,1,0:T(8,128)(2,1)S(1)} %collective-permute-done.22.refs_0_.refs_3_), channel_id=1, source_target_pairs={{0,16},{16,0},{1,17},{17,1},{2,18},{18,2},{3,19},{19,3},{4,20},{20... | collective-permute-start | bytes 2359304 | tf_op jit(solution)/shard_map/ppermute | solution.py:103
  212.5 48.5 %collective-permute-start.36 = (bf16[3,256,1024]{2,1,0:T(8,128)(2,1)}, bf16[3,256,1024]{2,1,0:T(8,128)(2,1)}, u32[]{:S(2)}, u32[]{:S(2)}) collective-permute-start(bf16[3,256,1024]{2,1,0:T(8,128)(2,1)} %get-tuple-element.670), channel_id=1, source_target_pairs={{0,4},{1,5},{4,8},{5,9},{8,12},{9,13},{12,14},{13,15},{14,10},{15,... | collective-permute-start | bytes 4718600 | tf_op jit(solution)/shard_map/ppermute | solution.py:94
  213.1 23.0 %collective-permute-start.33 = (bf16[3,128,1024]{2,1,0:T(8,128)(2,1)S(1)}, bf16[3,128,1024]{2,1,0:T(8,128)(2,1)S(1)}, u32[]{:S(2)}, u32[]{:S(2)}) collective-permute-start(bf16[3,128,1024]{2,1,0:T(8,128)(2,1)S(1)} %get-tuple-element.646), channel_id=1, source_target_pairs={{0,16},{16,0},{1,17},{17,1},{2,18},{18,2},{3,19},{19,3},{4,20},{20... | collective-permute-start | bytes 2359304 | tf_op jit(solution)/shard_map/ppermute | solution.py:103
  234.7 31.4 %collective-permute-start.34 = (bf16[3,128,1024]{2,1,0:T(8,128)(2,1)}, bf16[3,128,1024]{2,1,0:T(8,128)(2,1)}, u32[]{:S(2)}, u32[]{:S(2)}) collective-permute-start(bf16[3,128,1024]{2,1,0:T(8,128)(2,1)} %get-tuple-element.667), channel_id=1, source_target_pairs={{0,16},{16,0},{1,17},{17,1},{2,18},{18,2},{3,19},{19,3},{4,20},{20... | collective-permute-start | bytes 2359304 | tf_op jit(solution)/shard_map/ppermute | solution.py:103
  237.2 28.8 %collective-permute-start.35 = (bf16[3,128,1024]{2,1,0:T(8,128)(2,1)}, bf16[3,128,1024]{2,1,0:T(8,128)(2,1)}, u32[]{:S(2)}, u32[]{:S(2)}) collective-permute-start(bf16[3,128,1024]{2,1,0:T(8,128)(2,1)} %add_convert_fusion.9), channel_id=1, source_target_pairs={{4,0},{5,1},{8,4},{9,5},{12,8},{13,9},{14,12},{15,13},{10,14},{11,... | collective-permute-start | bytes 2359304 | tf_op jit(solution)/shard_map/ppermute | solution.py:97
  238.9 44.5 %collective-permute-start.41 = (bf16[256,2048]{1,0:T(8,128)(2,1)S(1)}, bf16[256,2048]{1,0:T(8,128)(2,1)}, u32[]{:S(2)}, u32[]{:S(2)}) collective-permute-start(bf16[256,2048]{1,0:T(8,128)(2,1)S(1)} %copy-done.13), channel_id=1, source_target_pairs={{0,1},{1,0},{2,3},{3,2},{4,5},{5,4},{6,7},{7,6},{8,9},{9,8},{10,11... | collective-permute-start | bytes 3145736 | tf_op jit(solution)/shard_map/ppermute | solution.py:100
  242.9 49.5 %collective-permute-start.38 = (bf16[3,128,1024]{2,1,0:T(8,128)(2,1)}, bf16[3,128,1024]{2,1,0:T(8,128)(2,1)}, u32[]{:S(2)}, u32[]{:S(2)}) collective-permute-start(bf16[3,128,1024]{2,1,0:T(8,128)(2,1)} %copy-done.42), channel_id=1, source_target_pairs={{0,16},{16,0},{1,17},{17,1},{2,18},{18,2},{3,19},{19,3},{4,20},{20... | collective-permute-start | bytes 2359304 | tf_op jit(solution)/shard_map/ppermute | solution.py:103
  265.3 49.3 %collective-permute-start.45 = (bf16[3,256,1024]{2,1,0:T(8,128)(2,1)}, bf16[3,256,1024]{2,1,0:T(8,128)(2,1)}, u32[]{:S(2)}, u32[]{:S(2)}) collective-permute-start(bf16[3,256,1024]{2,1,0:T(8,128)(2,1)} %add_convert_fusion.2), channel_id=1, source_target_pairs={{0,4},{1,5},{4,8},{5,9},{8,12},{9,13},{12,14},{13,15},{14,10},{15,... | collective-permute-start | bytes 4718600 | tf_op jit(solution)/shard_map/ppermute | solution.py:94
  283.3 21.5 %collective-permute-start.43 = (bf16[256,2560]{1,0:T(8,128)(2,1)}, bf16[256,2560]{1,0:T(8,128)(2,1)S(1)}, u32[]{:S(2)}, u32[]{:S(2)}) collective-permute-start(bf16[256,2560]{1,0:T(8,128)(2,1)} %copy-done.36), channel_id=1, source_target_pairs={{0,1},{1,0},{2,3},{3,2},{4,5},{5,4},{6,7},{7,6},{8,9},{9,8},{10,11... | collective-permute-start | bytes 3932168 | tf_op jit(solution)/shard_map/ppermute | solution.py:100
  286.9 20.9 %collective-permute-start.44 = (bf16[1024,512]{1,0:T(8,128)(2,1)S(1)}, bf16[1024,512]{1,0:T(8,128)(2,1)S(1)}, u32[]{:S(2)}, u32[]{:S(2)}) collective-permute-start(bf16[1024,512]{1,0:T(8,128)(2,1)S(1)} %convolution_convert_fusion.2), channel_id=1, source_target_pairs={{0,1},{1,0},{2,3},{3,2},{4,5},{5,4},{6,7},{7,6},{8,9},{9,8},{10,11... | collective-permute-start | bytes 3145736 | tf_op jit(solution)/shard_map/ppermute | solution.py:100
  292.3 30.1 %collective-permute-start.37 = (bf16[3,128,1024]{2,1,0:T(8,128)(2,1)S(1)}, bf16[3,128,1024]{2,1,0:T(8,128)(2,1)S(1)}, u32[]{:S(2)}, u32[]{:S(2)}) collective-permute-start(bf16[3,128,1024]{2,1,0:T(8,128)(2,1)S(1)} %copy-done.41), channel_id=1, source_target_pairs={{0,16},{16,0},{1,17},{17,1},{2,18},{18,2},{3,19},{19,3},{4,20},{20... | collective-permute-start | bytes 2359304 | tf_op jit(solution)/shard_map/ppermute | solution.py:103
  321.0 25.1 %collective-permute-start.60 = (bf16[32,5632]{1,0:T(8,128)(2,1)}, bf16[32,5632]{1,0:T(8,128)(2,1)}, u32[]{:S(2)}, u32[]{:S(2)}) collective-permute-start(bf16[32,5632]{1,0:T(8,128)(2,1)} %get-tuple-element.841), channel_id=1, source_target_pairs={{0,16},{16,0},{1,17},{17,1},{2,18},{18,2},{3,19},{19,3},{4,20},{20... | collective-permute-start | bytes 1081352 | tf_op jit(solution)/shard_map/ppermute | solution.py:103
  322.5 31.3 %collective-permute-start.55 = (bf16[32,5632]{1,0:T(8,128)(2,1)}, bf16[32,5632]{1,0:T(8,128)(2,1)}, u32[]{:S(2)}, u32[]{:S(2)}) collective-permute-start(bf16[32,5632]{1,0:T(8,128)(2,1)} %get-tuple-element.809), channel_id=1, source_target_pairs={{0,16},{16,0},{1,17},{17,1},{2,18},{18,2},{3,19},{19,3},{4,20},{20... | collective-permute-start | bytes 1081352 | tf_op jit(solution)/shard_map/ppermute | solution.py:103
  330.8 39.9 %collective-permute-start.48 = (bf16[3,128,1024]{2,1,0:T(8,128)(2,1)}, bf16[3,128,1024]{2,1,0:T(8,128)(2,1)}, u32[]{:S(2)}, u32[]{:S(2)}) collective-permute-start(bf16[3,128,1024]{2,1,0:T(8,128)(2,1)} %add_convert_fusion.6), channel_id=1, source_target_pairs={{4,0},{5,1},{8,4},{9,5},{12,8},{13,9},{14,12},{15,13},{10,14},{11,... | collective-permute-start | bytes 2359304 | tf_op jit(solution)/shard_map/ppermute | solution.py:97
  332.4 29.1 %collective-permute-start.64 = (bf16[32,5632]{1,0:T(8,128)(2,1)}, bf16[32,5632]{1,0:T(8,128)(2,1)}, u32[]{:S(2)}, u32[]{:S(2)}) collective-permute-start(bf16[32,5632]{1,0:T(8,128)(2,1)} %copy-done.43), channel_id=1, source_target_pairs={{0,16},{16,0},{1,17},{17,1},{2,18},{18,2},{3,19},{19,3},{4,20},{20... | collective-permute-start | bytes 1081352 | tf_op jit(solution)/shard_map/ppermute | solution.py:103
  338.3 30.9 %collective-permute-start.58 = (bf16[32,5632]{1,0:T(8,128)(2,1)S(1)}, bf16[32,5632]{1,0:T(8,128)(2,1)}, u32[]{:S(2)}, u32[]{:S(2)}) collective-permute-start(bf16[32,5632]{1,0:T(8,128)(2,1)S(1)} %get-tuple-element.825), channel_id=1, source_target_pairs={{0,16},{16,0},{1,17},{17,1},{2,18},{18,2},{3,19},{19,3},{4,20},{20... | collective-permute-start | bytes 1081352 | tf_op jit(solution)/shard_map/ppermute | solution.py:103
  346.0 61.9 %collective-permute-start.51 = (bf16[3,256,1024]{2,1,0:T(8,128)(2,1)}, bf16[3,256,1024]{2,1,0:T(8,128)(2,1)S(1)}, u32[]{:S(2)}, u32[]{:S(2)}) collective-permute-start(bf16[3,256,1024]{2,1,0:T(8,128)(2,1)} %add_convert_fusion.1), channel_id=1, source_target_pairs={{0,4},{1,5},{4,8},{5,9},{8,12},{9,13},{12,14},{13,15},{14,10},{15,... | collective-permute-start | bytes 4718600 | tf_op jit(solution)/shard_map/ppermute | solution.py:94
  353.8 33.8 %collective-permute-start.53 = (bf16[32,5632]{1,0:T(8,128)(2,1)S(1)}, bf16[32,5632]{1,0:T(8,128)(2,1)S(1)}, u32[]{:S(2)}, u32[]{:S(2)}) collective-permute-start(bf16[32,5632]{1,0:T(8,128)(2,1)S(1)} %get-tuple-element.787), channel_id=1, source_target_pairs={{0,16},{16,0},{1,17},{17,1},{2,18},{18,2},{3,19},{19,3},{4,20},{20... | collective-permute-start | bytes 1081352 | tf_op jit(solution)/shard_map/ppermute | solution.py:103
  361.5 76.2 %collective-permute-start.68 = (bf16[32,5632]{1,0:T(8,128)(2,1)}, bf16[32,5632]{1,0:T(8,128)(2,1)S(1)}, u32[]{:S(2)}, u32[]{:S(2)}) collective-permute-start(bf16[32,5632]{1,0:T(8,128)(2,1)} %get-tuple-element.872), channel_id=1, source_target_pairs={{0,16},{16,0},{1,17},{17,1},{2,18},{18,2},{3,19},{19,3},{4,20},{20... | collective-permute-start | bytes 1081352 | tf_op jit(solution)/shard_map/ppermute | solution.py:103
  385.9 23.0 %collective-permute-start.50 = (f32[39,1024]{1,0:T(8,128)S(1)}, f32[39,1024]{1,0:T(8,128)S(1)}, u32[]{:S(2)}, u32[]{:S(2)}) collective-permute-start(f32[39,1024]{1,0:T(8,128)S(1)} %add.280), channel_id=1, source_target_pairs={{0,1},{1,0},{2,3},{3,2},{4,5},{5,4},{6,7},{7,6},{8,9},{9,8},{10,11... | collective-permute-start | bytes 479240 | tf_op jit(solution)/shard_map/ppermute | solution.py:990
  416.7 21.0 %collective-permute-start.67 = (bf16[32,5632]{1,0:T(8,128)(2,1)S(1)}, bf16[32,5632]{1,0:T(8,128)(2,1)S(1)}, u32[]{:S(2)}, u32[]{:S(2)}) collective-permute-start(bf16[32,5632]{1,0:T(8,128)(2,1)S(1)} %add_convert_fusion.12), channel_id=1, source_target_pairs={{0,4},{1,5},{4,8},{5,9},{8,12},{9,13},{12,14},{13,15},{14,10},{15,... | collective-permute-start | bytes 1081352 | tf_op jit(solution)/shard_map/ppermute | solution.py:94
  418.5 23.5 %collective-permute-start.61 = (bf16[3,128,1024]{2,1,0:T(8,128)(2,1)S(1)}, bf16[3,128,1024]{2,1,0:T(8,128)(2,1)S(1)}, u32[]{:S(2)}, u32[]{:S(2)}) collective-permute-start(bf16[3,128,1024]{2,1,0:T(8,128)(2,1)S(1)} %get-tuple-element.845), channel_id=1, source_target_pairs={{0,16},{16,0},{1,17},{17,1},{2,18},{18,2},{3,19},{19,3},{4,20},{20... | collective-permute-start | bytes 2359304 | tf_op jit(solution)/shard_map/ppermute | solution.py:103
  (130 other events, 1543.3 us)
